TPU v7x, 32 devices: a whole 2x2x4 slice. The times are simulated.
32 devices in a mesh: seq: 32 (over z, y, x, core), mp: 1.
Axes of the slice: x: 2, y: 2, z: 4, core: 2. Of those that a mesh axis runs over, the one named last changes fastest.
Arguments:
- streams: float32 [4096, 3, 4096], P('seq', None, 'mp'), may hold values from -6 to 6
- se_filter: float32 [7, 3, 256], P(None, None, 'mp'), may hold values from -3 to 3
- mr_filter: float32 [128, 256], P(None, 'mp'), may hold values from -1.5 to 1.5
- mr_decay: float32 [256], P('mp'), may hold values from 0.004 to 0.1
- query: float32 [4096, 4096], P('seq', 'mp'), may hold values from -8 to 8
- key: float32 [4096, 4096], P('seq', 'mp'), may hold values from -8 to 8
- value: float32 [4096, 4096], P('seq', 'mp'), may hold values from -6 to 6
- placement_list: int32 [32], replicated, may hold values from 0 to 31, each once
- doc_ids: int32 [4096], replicated, may hold values from 0 to 7, never falling along the last dimension, each value on 1 to 1024 neighbouring positions
- norm_gain: float32 [4096], P('mp'), may hold values from 0.25 to 1.75
Outputs:
- mixed: float32 [4096, 4096], P('seq', 'mp')
Inputs may be any that keep to these rules, and one draw needn't show every extreme that they name: placement_list names every stretch once. doc_ids never falls along the sequence; each document holds at most 1024 positions and one holds exactly that many.
All inputs are finite; a program needn't handle non-finite values.
Results may differ from a plain program's by a relative error of at most 0.0003.
Values sent between devices are 32-bit elements; how exact they have to be, the bound alone decides.
A program may use at most 576 MiB of HBM per device.

v0:
```python
import jax
import jax.numpy as jnp
from jax import lax
from jax.sharding import PartitionSpec as P

HD = 128


def per_device(
    streams, se_filter, mr_filter, mr_decay, query, key, value, placement_list, doc_ids, norm_gain
):
    tok = streams.shape[0]
    chl = streams.shape[2]
    groups_l = se_filter.shape[2]
    group_w = chl // groups_l
    se_len = se_filter.shape[0]
    mr_len = mr_filter.shape[0]
    heads_l = chl // HD
    seq_count = placement_list.shape[0]
    device = lax.axis_index("seq")
    stretch = placement_list[device]
    listing = jnp.arange(seq_count, dtype=jnp.int32)
    source = jnp.sum(jnp.where(placement_list == stretch - 1, listing, 0))
    base = stretch * tok
    offsets = jnp.arange(tok, dtype=jnp.int32)
    local_pos = base + offsets
    local_doc = lax.dynamic_slice_in_dim(doc_ids, base, tok)

    def earlier_docs(width):
        where_pos = base - width + jnp.arange(width, dtype=jnp.int32)
        found = doc_ids[jnp.clip(where_pos, 0, doc_ids.shape[0] - 1)]
        return jnp.where(where_pos >= 0, found, -1)

    def pick(piece):
        owner = jnp.arange(piece.shape[0], dtype=jnp.int32) == source
        mask = owner.reshape((piece.shape[0],) + (1,) * (piece.ndim - 1))
        return jnp.sum(jnp.where(mask, piece, 0.0), axis=0)

    short_tail = pick(
        lax.all_gather(streams[tok - (se_len - 1) :][None], "seq", axis=0, tiled=True)
    )
    extended = jnp.concatenate([short_tail, streams], axis=0)
    ext_doc = jnp.concatenate([earlier_docs(se_len - 1), local_doc])
    short_taps = jnp.repeat(se_filter, group_w, axis=2)
    featured = jnp.zeros((tok, 3, chl), jnp.float32)
    for lag in range(se_len):
        first = se_len - 1 - lag
        same = (ext_doc[first : first + tok] == local_doc)[:, None, None]
        featured = featured + jnp.where(
            same, short_taps[lag][None] * extended[first : first + tok], 0.0
        )
    gated = featured[:, 1] * featured[:, 2]
    decays = jnp.arange(mr_len, dtype=jnp.float32)[:, None]
    taps = mr_filter * jnp.exp(-mr_decay[None, :] * decays)
    scale = 1.0 / jnp.sqrt(jnp.float32(HD))
    tail_piece = gated[tok - (mr_len - 1) :][None]
    long_tail = pick(lax.all_gather(tail_piece, "seq", axis=0, tiled=True))
    q_heads = query.reshape(tok, heads_l, HD)
    key_pos = (placement_list[:, None] * tok + offsets[None, :]).reshape(-1)
    key_doc = doc_ids[jnp.clip(key_pos, 0, doc_ids.shape[0] - 1)]
    allowed = (
        (key_pos >= 0)[None, :]
        & (key_pos[None, :] <= local_pos[:, None])
        & (key_doc[None, :] == local_doc[:, None])
    )[None]
    k_heads = lax.all_gather(key[None], "seq", axis=0, tiled=True).reshape(-1, heads_l, HD)
    v_heads = lax.all_gather(value[None], "seq", axis=0, tiled=True).reshape(-1, heads_l, HD)
    top_old = jnp.full((heads_l, tok), -1e30, jnp.float32)
    scores = jnp.einsum("qhd,khd->hqk", q_heads, k_heads, precision=lax.Precision.HIGHEST) * scale
    scores = jnp.where(allowed, scores, jnp.float32(-1e30))
    top_new = jnp.maximum(top_old, jnp.max(scores, axis=2))
    weights = jnp.where(allowed, jnp.exp(scores - top_new[:, :, None]), 0.0)
    total_new = jnp.sum(weights, axis=2)
    acc_new = jnp.einsum("hqk,khd->hqd", weights, v_heads, precision=lax.Precision.HIGHEST)
    attended = (acc_new / total_new[:, :, None]).transpose(1, 0, 2).reshape(tok, chl)
    span = tok + mr_len - 1
    ext_rows = jnp.concatenate([long_tail, gated], axis=0)
    doc_rows = jnp.concatenate([earlier_docs(mr_len - 1), local_doc])
    lag = (
        jnp.arange(tok, dtype=jnp.int32)[:, None]
        + (mr_len - 1)
        - jnp.arange(span, dtype=jnp.int32)[None, :]
    )
    valid = (lag >= 0) & (lag < mr_len) & (doc_rows[None, :] == local_doc[:, None])
    toeplitz = jnp.where(valid[:, :, None], taps[jnp.clip(lag, 0, mr_len - 1)], 0.0)
    conv = jnp.einsum(
        "tsg,sgc->tgc",
        toeplitz,
        ext_rows.reshape(span, groups_l, group_w),
        precision=lax.Precision.HIGHEST,
    ).reshape(tok, chl)
    hyena = featured[:, 0] * conv
    summed = hyena + attended
    row_squares = lax.psum(jnp.sum(summed * summed, axis=1), "mp")
    norm_scale = lax.rsqrt(row_squares / (chl * lax.axis_size("mp")) + 1e-05)
    return summed * norm_scale[:, None] * norm_gain[None, :]


def solution(mesh):
    placed = (
        P("seq", None, "mp"),
        P(None, None, "mp"),
        P(None, "mp"),
        P("mp"),
        P("seq", "mp"),
        P("seq", "mp"),
        P("seq", "mp"),
        P(),
        P(),
        P("mp"),
    )
    return jax.shard_map(
        per_device, mesh=mesh, in_specs=placed, out_specs=P("seq", "mp"), check_vma=False
    )
```

profile of v0, /device:TPU:0, one launch (start us, length us, event | category | flops | bytes accessed | tf_op | source)
XLA Modules:
  0.0 1899.7 jit_solution(2272746300996746089)
XLA Ops:
  6.6 1.2 slice.140
  7.8 0.9 copy.86
  8.8 0.7 all-gather.15.cloned.1.call-update
  9.5 2.9 copy.50
  12.4 0.0 all-gather.11.cloned.1.call-start
  12.5 0.7 dynamic_slice.6
  13.9 0.6 gather_fusion
  14.5 0.1 dynamic_slice.7
  14.7 0.2 broadcast_in_dim.193
  14.8 0.2 broadcast_in_dim.194
  15.1 0.2 broadcast_in_dim.201
  15.2 0.2 broadcast_in_dim.202
  15.5 0.2 broadcast_in_dim.204
  15.7 0.2 broadcast_in_dim.205
  15.9 0.2 broadcast_in_dim.207
  16.1 0.2 broadcast_in_dim.208
  16.3 0.2 broadcast_in_dim.210
  16.5 0.2 broadcast_in_dim.211
  16.7 0.2 broadcast_in_dim.213
  16.9 0.2 broadcast_in_dim.214
  17.8 0.2 broadcast_in_dim.189
  18.0 0.2 broadcast_in_dim.190
  18.2 1.1 fusion.37
  19.4 0.6 iota_compare_fusion
  20.0 0.1 pad_add_fusion
  20.1 0.1 slice_compare_fusion.5
  20.2 88.8 %all-gather.9.cloned.1.call-done = f32[192,3,4096]{2,1,0:T(4,128)} async-done(((f32[6,3,4096]{2,1,0:T(4,128)}), f32[192,3,4096]{2,1,0:T(4,128)}) %all-gather.9.cloned.1.call-update) | async-done | bytes 9437200 | tf_op jit(solution)/shard_map/all_gather | solution.py:40
  108.9 11.0 fusion.8
  120.0 0.9 copy_dynamic-update-slice_fusion
  120.9 11.8 copy_dynamic-update-slice_fusion.1
  132.7 25.3 %fusion.10 = f32[128,3,4096]{2,1,0:T(4,128)S(1)} fusion(f32[134,3,4096]{2,1,0:T(4,128)} %copy_dynamic-update-slice_fusion.1, f32[3,4096]{1,0:T(4,128)S(1)} %broadcast_in_dim.214, f32[3,4096]{1,0:T(4,128)S(1)} %broadcast_in_dim.211, f32[3,4096]{1,0:T(4,128)S(1)} %broadcast_in_dim.208, f32[3,4096]{1,0:T(4,128)S(1)} %broadcast_in_dim.205, ...), kind=kLoop, calls=%fused_computation.20 | loop fusion | flops 29884416 | bytes 50676480 | tf_op jit(solution)/shard_map/add | solution.py:49
  158.0 4.9 fusion.44
  162.9 1.3 copy-done.3
  164.2 1.5 slice.150
  165.8 1.1 gather_fusion.1
  166.9 0.1 compare_select_fusion
  167.0 0.3 reshape.378
  167.5 77.3 %gather_fusion.2 = f32[32640,256]{1,0:T(8,128)} fusion(f32[128,256]{1,0:T(8,128)S(1)} %exponential_multiply_fusion, s32[32768]{0:T(1024)S(1)} %pad_clamp_fusion), kind=kCustom, calls=%fused_computation.2 | custom fusion | bytes 66977280 | tf_op jit(solution)/shard_map/gather | solution.py:85
  244.8 27.8 %reshape.377 = f32[128,255,256]{2,1,0:T(8,128)} reshape(f32[32640,256]{1,0:T(8,128)} %gather_fusion.2) | data formatting | bytes 66846720 | tf_op jit(solution)/shard_map/gather | solution.py:85
  272.6 0.1 pad_add_fusion.1
  272.7 0.1 fusion.34
  272.8 27.1 %broadcast_select_fusion = f32[128,255,256]{2,1,0:T(8,128)} fusion(f32[128,255,256]{2,1,0:T(8,128)} %reshape.377, pred[128,255]{1,0:T(8,128)(4,1)S(1)} %fusion.34), kind=kLoop, calls=%fused_computation.15 | loop fusion | flops 8355840 | bytes 66879360 | tf_op jit(solution)/shard_map/jit(_where)/select_n | solution.py:85
  299.9 34.2 %copy.48 = f32[128,255,256]{1,0,2:T(8,128)} copy(f32[128,255,256]{2,1,0:T(8,128)} %broadcast_select_fusion) | data formatting | bytes 66846720 | tf_op jit(solution)/shard_map/jit(_where)/select_n | solution.py:85
  334.1 0.1 fusion.36
  334.2 23.0 %gather_fusion.3 = s32[4096]{0:T(1024)S(1)} fusion(s32[4096]{0:T(1024)S(1)} %copy-done.2, s32[4096]{0:T(1024)S(1)} %broadcast_clamp_fusion), kind=kCustom, calls=%fused_computation.3 | custom fusion | bytes 49152 | tf_op jit(solution)/shard_map/gather | solution.py:60
  357.2 0.1 broadcast_compare_fusion
  357.3 0.6 compare_and_fusion
  357.9 5.6 copy.47
  363.6 5.6 copy.55
  369.2 97.1 %all-gather.15.cloned.1.call-done = f32[4096,4096]{1,0:T(8,128)} async-done(((f32[128,4096]{1,0:T(8,128)}), f32[4096,4096]{1,0:T(8,128)}) %all-gather.15.cloned.1.call-update) | async-done | bytes 67108880 | tf_op jit(solution)/shard_map/all_gather | solution.py:67
  466.3 66.3 %copy.53 = f32[4096,4096]{0,1:T(8,128)} copy(f32[4096,4096]{1,0:T(8,128)} %all-gather.15.cloned.1.call-done) | data formatting | bytes 134217728 | tf_op jit(solution)/shard_map/all_gather | solution.py:67
  532.6 291.2 %all-gather.13.cloned.1.call-done = f32[4096,4096]{0,1:T(8,128)} async-done(((f32[128,4096]{0,1:T(8,128)}), f32[4096,4096]{0,1:T(8,128)}) %all-gather.13.cloned.1.call-update) | async-done | bytes 67108880 | tf_op jit(solution)/shard_map/all_gather | solution.py:66
  823.8 79.7 %fusion = (f32[32,128]{1,0:T(8,128)S(1)}, f32[32,128,4096]{2,1,0:T(8,128)}) fusion(pred[128,4096]{1,0:T(8,128)(4,1)S(1)} %compare_and_fusion, f32[4096,32,128]{0,2,1:T(8,128)} %bitcast.12, f32[128,4096]{1,0:T(8,128)S(1)} %copy-done), kind=kOutput, calls=%fused_computation.7 | convolution fusion | flops 25820131328 | bytes 136855552 | tf_op jit(solution)/shard_map/qhd,khd->hqk/dot_general | solution.py:69
  903.5 23.9 %fusion.1 = f32[32,128]{1,0:T(8,128)S(1)} fusion(f32[32,128,4096]{2,1,0:T(8,128)} %get-tuple-element.25, f32[32,128]{1,0:T(8,128)S(1)} %broadcast_maximum_fusion, pred[128,4096]{1,0:T(8,128)(4,1)S(1)} %compare_and_fusion), kind=kLoop, calls=%fused_computation.8 | loop fusion | flops 83881984 | bytes 67665920 | tf_op jit(solution)/shard_map/reduce_sum | solution.py:73
  927.4 250.7 %all-gather.11.cloned.1.call-done = f32[4064,1,4096]{2,1,0:T(1,128)} async-done(((f32[127,1,4096]{2,1,0:T(1,128)}), f32[4064,1,4096]{2,1,0:T(1,128)}) %all-gather.11.cloned.1.call-update) | async-done | bytes 66584592 | tf_op jit(solution)/shard_map/all_gather | solution.py:57
  1178.1 504.2 %reduce.1 = f32[4064,4096]{1,0:T(8,128)} reduce(f32[4064,1,4096]{2,1,0:T(1,128)} %all-gather.11.cloned.1.call-done, f32[]{:T(128)} %constant.14), dimensions={1}, to_apply=%all-gather.1.reduce_sub_computation | reduce | bytes 133169152 | tf_op jit(solution)/shard_map/all_gather | solution.py:57
  1682.2 53.9 %reshape.393 = f32[32,127,4096]{2,1,0:T(8,128)} reshape(f32[4064,4096]{1,0:T(8,128)} %reduce.1) | data formatting | bytes 133169152 | tf_op jit(solution)/shard_map/all_gather | solution.py:57
  1736.2 21.2 %select_reduce_fusion = f32[127,4096]{1,0:T(8,128)S(1)} fusion(f32[32,127,4096]{2,1,0:T(8,128)} %reshape.393, pred[32]{0:T(512)(128)(4,1)S(1)} %copy-done.10), kind=kLoop, calls=%fused_computation.6 | loop fusion | flops 32772096 | bytes 68665376 | tf_op jit(solution)/shard_map/reduce_sum | solution.py:37
  1757.3 1.9 copy.46
  1759.2 32.8 %fusion.21 = f32[256,16,128]{2,1,0:T(8,128)S(1)} fusion(f32[128,255,256]{1,0,2:T(8,128)} %copy.48, f32[128,256,16]{0,2,1:T(8,128)} %bitcast.75, f32[127,256,16]{0,2,1:T(8,128)} %bitcast.76), kind=kOutput, calls=%fused_computation.36 | convolution fusion | flops 1605365760 | bytes 39698432 | tf_op jit(solution)/shard_map/tsg,sgc->tgc/dot_general | solution.py:86
  1791.9 88.9 %multiply_reduce_fusion = (f32[128]{0:T(128)S(1)}, f32[128,32,128]{0,2,1:T(8,128)}) fusion(f32[128,32,128]{0,2,1:T(8,128)} %bitcast.77, f32[128,32,128]{0,2,1:T(8,128)S(1)} %bitcast.72, f32[128,32]{0,1:T(8,128)S(1)} %bitcast.82, f32[4096,32,128]{0,2,1:T(8,128)} %bitcast.13, f32[32,128,4096]{2,1,0:T(8,128)} %get-tuple-element.25, ...), kind=kOutput, calls=%fused_computation.49 | convolution fusion | flops 25839534080 | bytes 141066752 | tf_op jit(solution)/shard_map/hqk,khd->hqd/dot_general | solution.py:74
  1880.8 3.1 copy.54
  1883.9 2.9 copy.49
  1886.8 6.2 fusion.30
  (55 shorter events, 0.4 us)
Async XLA Ops:
  6.5 817.3 %copy-start = (f32[128,4096]{1,0:T(8,128)S(1)}, f32[128,4096]{1,0:T(8,128)}, u32[]{:S(2)}) copy-start(f32[128,4096]{1,0:T(8,128)} %param.14) | copy-start | bytes 6291460
  6.5 6.0 copy-start.12
  6.5 7.4 copy-start.2
  6.5 8.1 copy-start.6
  6.5 102.4 %all-gather.9.cloned.1.call-start = ((), (), s32[]{:S(2)}) async-start(), calls=%async_computation | async-start | bytes 12976128 | tf_op jit(solution)/shard_map/all_gather | solution.py:40
  8.7 457.6 %all-gather.15.cloned.1.call-start = ((), (), s32[]{:S(2)}) async-start(), calls=%async_computation.3 | async-start | bytes 69206016 | tf_op jit(solution)/shard_map/all_gather | solution.py:67
  9.5 814.3 %all-gather.13.cloned.1.call-start = ((), (), s32[]{:S(2)}) async-start(), calls=%async_computation.2 | async-start | bytes 69206016 | tf_op jit(solution)/shard_map/all_gather | solution.py:66
  12.4 1165.6 %all-gather.11.cloned.1.call-start = ((), (), s32[]{:S(2)}) async-start(), calls=%async_computation.1 | async-start | bytes 68665344 | tf_op jit(solution)/shard_map/all_gather | solution.py:57
  20.0 112.7 %copy-start.9 = (pred[32]{0:T(512)(128)(4,1)}, pred[32]{0:T(512)(128)(4,1)S(1)}, u32[]{:S(2)}) copy-start(pred[32]{0:T(512)(128)(4,1)S(1)} %iota_compare_fusion) | copy-start | bytes 100
  120.0 12.8 slice-start
  120.9 11.8 slice-start.1
  158.0 9.4 copy-start.11
  158.0 9.4 copy-start.5
  162.9 1.3 copy-start.3
  299.9 34.2 %copy-start.8 = (s32[32]{0:T(128)S(1)}, s32[32]{0:T(128)}, u32[]{:S(2)}) copy-start(s32[32]{0:T(128)} %get-tuple-element.21) | copy-start | bytes 388
  1682.2 53.9 %copy-start.10 = (pred[32]{0:T(512)(128)(4,1)S(1)}, pred[32]{0:T(512)(128)(4,1)}, u32[]{:S(2)}) copy-start(pred[32]{0:T(512)(128)(4,1)} %copy-done.9) | copy-start | bytes 100
  1791.9 88.9 %copy-start.4 = (f32[256,16,128]{2,1,0:T(8,128)}, f32[256,16,128]{2,1,0:T(8,128)S(1)}, u32[]{:S(2)}) copy-start(f32[256,16,128]{2,1,0:T(8,128)S(1)} %fusion.21) | copy-start | bytes 6291460
  1880.8 6.0 copy-start.7
  1880.8 12.2 copy-start.1
Sparse Core Ops, SparseCore 0:
  10.2 98.6 all-gather.8
  111.8 354.5 all-gather.14
  467.9 355.9 all-gather.12
  826.5 351.4 all-gather.10
where the time goes:
time: 1910 us; the launch traced here: 1900 us
  waiting for transfers between devices  729 us (38%)
  other arithmetic  627 us (33%)
  local copies, waits for them, and re-layouts  328 us (17%)
  matrix products  201 us (11%)
    all_gather x1, other arithmetic, per_device(): long_tail = pick(lax.all_gather(tail_piece, 'seq', axis=0, tiled=True))  504 us
    all_gather x1, waiting for transfers between devices, per_device(): lax.all_gather(key[None], 'seq', axis=0, tiled=True)  291 us
    all_gather x1, waiting for transfers between devices, per_device(): long_tail = pick(lax.all_gather(tail_piece, 'seq', axis=0, tiled=True))  251 us
    gather x2, local copies, waits for them, and re-layouts, per_device(): taps[jnp.clip(lag, 0, mr_len - 1)]  105 us
    all_gather x1, waiting for transfers between devices, per_device(): lax.all_gather(value[None], 'seq', axis=0, tiled=True)  97.1 us
    dot_general x1, matrix products, per_device(): jnp.einsum('hqk,khd->hqd', weights, v_heads, precision=lax.Precision.HIGH...  88.9 us
    all_gather x1, waiting for transfers between devices, per_device(): lax.all_gather(streams[tok - (se_len - 1):][None], 'seq', axis=0, tiled=T...  88.8 us
    dot_general x1, matrix products, per_device(): jnp.einsum('qhd,khd->hqk', q_heads, k_heads, precision=lax.Precision.HIGH...  79.7 us
  transfers between devices with their start and end apart: 4, of which 4 were waited for; matrix products, arithmetic and copies ran while one was open for 23% of the time, Pallas kernels for 0%

commit v1 on v0

--- a/solution.py
+++ b/solution.py
@@ -1,12 +1,258 @@
+import functools
+
 import jax
 import jax.numpy as jnp
 from jax import lax
+from jax.experimental import pallas as pl
+from jax.experimental.pallas import tpu as pltpu
 from jax.sharding import PartitionSpec as P
 
 HD = 128
-
-
-def per_device(
+TILE = 256
+NT = (((1,), (1,)), ((), ()))
+
+
+def halves(x):
+    high = x.astype(jnp.bfloat16)
+    return high, (x - high.astype(jnp.float32)).astype(jnp.bfloat16)
+
+
+def mul(a, b):
+    return jnp.dot(a, b, preferred_element_type=jnp.float32)
+
+
+def hyena_kernel(
+    group_w, inv_ref, doc_ref, s_ref, short_ref, long_ref, docs_ref, place_ref, out_ref,
+    ext, window, long_hi, long_lo,
+):
+    count, streams, tok, width = s_ref.shape
+    lags = short_ref.shape[0]
+    groups = width // group_w
+    lead = ext.shape[1] - tok
+    long_hi[...], long_lo[...] = halves(long_ref[...])
+    ext[...] = jnp.zeros_like(ext)
+    window[...] = jnp.zeros_like(window)
+    lane_group = lax.broadcasted_iota(jnp.int32, (tok, width), 1) // group_w
+
+    def stretch(c, carry):
+        b = inv_ref[c]
+        place = place_ref[pl.ds(pl.multiple_of(c * tok, tok), tok), :]
+        for j in range(streams):
+            ext[j, :lead] = ext[j, tok:]
+            ext[j, lead:] = s_ref[b, j]
+        featured = []
+        for j in range(streams):
+            total = short_ref[0, j][None, :] * ext[j, lead:]
+            for lag in range(1, lags):
+                term = short_ref[lag, j][None, :] * ext[j, lead - lag : lead - lag + tok]
+                total = total + jnp.where(place >= lag, term, 0.0)
+            featured.append(total)
+        window[:tok] = window[tok:]
+        window[tok:] = featured[1] * featured[2]
+        docs = docs_ref[pl.ds(pl.multiple_of(c * tok, tok), 2 * tok), :]
+
+        def document(d, conv):
+            hi, lo = halves(jnp.where(docs == d, window[...], 0.0))
+            both = mul(long_hi[...], jnp.concatenate([hi, lo], axis=1))
+            full = both[:, :width] + both[:, width:] + mul(long_lo[...], hi)
+            part = jnp.zeros((tok, width), jnp.float32)
+            for g in range(groups):
+                part = jnp.where(lane_group == g, full[g * tok : (g + 1) * tok], part)
+            return jnp.where(docs[tok:] == d, part, conv)
+
+        conv = lax.fori_loop(
+            doc_ref[c * tok],
+            doc_ref[c * tok + tok - 1] + 1,
+            document,
+            jnp.zeros((tok, width), jnp.float32),
+        )
+        out_ref[b] = featured[0] * conv
+        return carry
+
+    lax.fori_loop(0, count, stretch, 0)
+
+
+def attention_kernel(
+    scale, inv_ref, start_ref, x_ref, hyena_ref, starts_ref, out_ref, keys, values
+):
+    count, _, tok, width = x_ref.shape
+    per = TILE // tok
+
+    def prepare(c, carry):
+        rows = pl.ds(pl.multiple_of(c * tok, tok), tok)
+        b = inv_ref[c]
+        keys[rows, :] = jnp.concatenate(halves(x_ref[b, 1]), axis=1)
+        values[rows, :] = jnp.concatenate(halves(x_ref[b, 2]), axis=1)
+        return carry
+
+    lax.fori_loop(0, count, prepare, 0)
+
+    def rows_of(i, carry):
+        stored = [inv_ref[i * per + r] for r in range(per)]
+        q = jnp.concatenate([x_ref[b, 0] for b in stored], axis=0) * scale
+        q_hi, q_lo = halves(q)
+        q_both = jnp.concatenate([q_hi, q_hi], axis=1)
+        starts = starts_ref[pl.ds(pl.multiple_of(i * TILE, TILE), TILE), :]
+        row = i * TILE + lax.broadcasted_iota(jnp.int32, (TILE, TILE), 0)
+        lane = lax.broadcasted_iota(jnp.int32, (TILE, TILE), 1)
+
+        def block(j, carry):
+            top, total, acc = carry
+            rows = pl.ds(pl.multiple_of(j * TILE, TILE), TILE)
+            k = keys[rows, :]
+            s = lax.dot_general(q_both, k, NT, preferred_element_type=jnp.float32)
+            s = s + lax.dot_general(q_lo, k[:, :width], NT, preferred_element_type=jnp.float32)
+            col = j * TILE + lane
+            allowed = (col >= starts) & (col <= row)
+            s = jnp.where(allowed, s, -1e30)
+            new = jnp.maximum(top, jnp.max(s, axis=1, keepdims=True))
+            w = jnp.where(allowed, jnp.exp(s - new), 0.0)
+            fade = jnp.exp(top - new)
+            w_hi, w_lo = halves(w)
+            v = values[rows, :]
+            both = mul(w_hi, v)
+            got = both[:, :width] + both[:, width:] + mul(w_lo, v[:, :width])
+            return new, fade * total + jnp.sum(w, axis=1, keepdims=True), fade * acc + got
+
+        first = lax.div(start_ref[i * TILE], TILE)
+        top, total, acc = lax.fori_loop(
+            first,
+            i + 1,
+            block,
+            (
+                jnp.full((TILE, 1), -1e30, jnp.float32),
+                jnp.zeros((TILE, 1), jnp.float32),
+                jnp.zeros((TILE, width), jnp.float32),
+            ),
+        )
+        attended = acc / total
+        for r, b in enumerate(stored):
+            out_ref[b] = attended[r * tok : (r + 1) * tok] + hyena_ref[b]
+        return carry
+
+    lax.fori_loop(0, count // per, rows_of, 0)
+
+
+def split_heads(
+    streams, se_filter, mr_filter, mr_decay, query, key, value, placement_list, doc_ids, norm_gain
+):
+    tok, kinds, chl = streams.shape
+    se_len, _, groups_l = se_filter.shape
+    mr_len = mr_filter.shape[0]
+    count = placement_list.shape[0]
+    group_w = chl // groups_l
+    width = chl // count
+    groups = groups_l // count
+    tokens = count * tok
+    me = lax.axis_index("seq")
+    index = jnp.arange(count, dtype=jnp.int32)
+    inverse = jnp.sum(
+        jnp.where(placement_list[None, :] == index[:, None], index[None, :], 0), axis=1
+    )
+    positions = jnp.arange(tokens, dtype=jnp.int32)
+    fresh = jnp.concatenate([jnp.ones((1,), bool), doc_ids[1:] != doc_ids[:-1]])
+    starts = lax.cummax(jnp.where(fresh, positions, 0))
+    docs = jnp.concatenate([jnp.full((tok,), -1, jnp.int32), doc_ids])
+
+    def exchange(x):
+        return lax.all_to_all(x, "seq", 0, 0, tiled=True)
+
+    with jax.named_scope("streams_to_channels"):
+        sent = streams.reshape(tok, kinds, count, width).transpose(2, 1, 0, 3)
+        by_channel = exchange(sent)
+    with jax.named_scope("qkv_to_heads"):
+        stacked = jnp.stack([query, key, value], axis=0).reshape(3, tok, count, width)
+        by_head = exchange(stacked.transpose(2, 0, 1, 3))
+
+    with jax.named_scope("filters"):
+        short = lax.dynamic_slice_in_dim(se_filter, me * groups, groups, 2)
+        short = jnp.repeat(short, group_w, axis=2)
+        decays = jnp.arange(mr_len, dtype=jnp.float32)[:, None]
+        taps = lax.dynamic_slice_in_dim(mr_filter, me * groups, groups, 1)
+        decay = lax.dynamic_slice_in_dim(mr_decay, me * groups, groups, 0)
+        taps = (taps * jnp.exp(-decay[None, :] * decays)).T
+        period = 3 * tok
+        line = jnp.concatenate(
+            [
+                jnp.zeros((groups, tok - mr_len + 1), jnp.float32),
+                taps[:, ::-1],
+                jnp.zeros((groups, period - tok - 1), jnp.float32),
+            ],
+            axis=1,
+        )
+        sheared = jnp.tile(line, (1, tok))[:, : tok * (period - 1)]
+        long = sheared.reshape(groups, tok, period - 1)[:, :, : 2 * tok]
+        long = long.reshape(groups * tok, 2 * tok)
+
+    smem = pl.BlockSpec(memory_space=pltpu.SMEM)
+    vmem = pl.BlockSpec(memory_space=pltpu.VMEM)
+    shape = jax.ShapeDtypeStruct((count, tok, width), jnp.float32)
+    params = pltpu.CompilerParams(vmem_limit_bytes=56 * 2**20)
+    hyena = pl.pallas_call(
+        functools.partial(hyena_kernel, group_w),
+        out_shape=shape,
+        in_specs=[smem, smem, vmem, vmem, vmem, vmem, vmem],
+        out_specs=vmem,
+        scratch_shapes=[
+            pltpu.VMEM((kinds, tok + 8, width), jnp.float32),
+            pltpu.VMEM((2 * tok, width), jnp.float32),
+            pltpu.VMEM((groups * tok, 2 * tok), jnp.bfloat16),
+            pltpu.VMEM((groups * tok, 2 * tok), jnp.bfloat16),
+        ],
+        compiler_params=params,
+        cost_estimate=pl.CostEstimate(
+            flops=40 * 6 * groups * tok * 2 * tok * width, bytes_accessed=12 * 2**20,
+            transcendentals=0,
+        ),
+        name="hyena",
+    )(
+        inverse, doc_ids, by_channel, short, long, docs[:, None], (positions - starts)[:, None]
+    )
+    summed = pl.pallas_call(
+        functools.partial(attention_kernel, 1.0 / HD**0.5),
+        out_shape=shape,
+        in_specs=[smem, smem, vmem, vmem, vmem],
+        out_specs=vmem,
+        scratch_shapes=[
+            pltpu.VMEM((tokens, 2 * width), jnp.bfloat16),
+            pltpu.VMEM((tokens, 2 * width), jnp.bfloat16),
+        ],
+        compiler_params=params,
+        cost_estimate=pl.CostEstimate(
+            flops=12 * tokens * 1024 * width, bytes_accessed=12 * 2**20,
+            transcendentals=tokens * 1024,
+        ),
+        name="attention",
+    )(inverse, starts, by_head, hyena, starts[:, None])
+    with jax.named_scope("back_to_tokens"):
+        back = exchange(summed)
+        summed = back.transpose(1, 0, 2).reshape(tok, chl)
+    row_squares = lax.psum(jnp.sum(summed * summed, axis=1), "mp")
+    norm_scale = lax.rsqrt(row_squares / (chl * lax.axis_size("mp")) + 1e-05)
+    return summed * norm_scale[:, None] * norm_gain[None, :]
+
+
+def fits(tok, chl, groups_l, se_len, mr_len, count):
+    return (
+        chl == count * HD
+        and groups_l % count == 0
+        and TILE % tok == 0
+        and tok >= 128
+        and (count * tok) % TILE == 0
+        and mr_len <= tok
+        and se_len <= 9
+    )
+
+
+def per_device(*args):
+    streams, se_filter, mr_filter = args[:3]
+    sizes = (streams.shape[0], streams.shape[2], se_filter.shape[2])
+    if fits(*sizes, se_filter.shape[0], mr_filter.shape[0], args[7].shape[0]):
+        return split_heads(*args)
+    return gather_all(*args)
+
+
+def gather_all(
     streams, se_filter, mr_filter, mr_decay, query, key, value, placement_list, doc_ids, norm_gain
 ):
     tok = streams.shape[0]

time: 1910 us -> 398 us (0.21)
  other arithmetic: 627 us -> 11.1 us
  waiting for transfers between devices: 729 us -> 217 us
  local copies, waits for them, and re-layouts: 328 us -> 37.2 us
  matrix products: 201 us -> 0 us
  Pallas kernels: 0 us -> 69.8 us
  blocking collectives: 0 us -> 51.5 us
    all_gather x4 -> x0, waiting for transfers between devices: 728 us -> none  [the longest x1 291 us: per_device(): lax.all_gather(key[None], 'seq', axis=0, tiled=True)]
    all_gather x1 -> x0, other arithmetic: 504 us -> none  [per_device(): long_tail = pick(lax.all_gather(tail_piece, 'seq', axis=0, tiled=True))]
    all_to_all x0 -> x2, waiting for transfers between devices: none -> 217 us  [exchange(): return lax.all_to_all(x, 'seq', 0, 0, tiled=True)]
    dot_general x3 -> x0, matrix products: 201 us -> none  [the longest x1 88.9 us: per_device(): jnp.einsum('hqk,khd->hqd', weights, v_heads, precision=lax.Precision.HIGH...]
    gather x5 -> x0, local copies, waits for them, and re-layouts: 130 us -> none  [the longest x2 105 us: per_device(): taps[jnp.clip(lag, 0, mr_len - 1)]]
    all_gather x2 -> x0, local copies, waits for them, and re-layouts: 120 us -> none  [the longest x1 66.3 us: per_device(): lax.all_gather(value[None], 'seq', axis=0, tiled=True)]
    pallas_call x0 -> x2, Pallas kernels: none -> 69.8 us  [the longest x1 36.4 us: split_heads(): pl.pallas_call(functools.partial(attention_kernel, 1.0 / HD ** 0.5), out_...]
    reduce_sum x4 -> x2, other arithmetic: 57.2 us -> 0.94 us  [the longest x1 0.7 us: split_heads(): jnp.sum(jnp.where(placement_list[None, :] == index[:, None], index[None,...]
  transfers between devices with their start and end apart: 4 -> 2, of which waited for: 4 -> 2; matrix products, arithmetic and copies ran while one was open for 23% -> 7% of each run, Pallas kernels for 0% -> 8%
where the time goes in v1:
time: 398 us
  waiting for transfers between devices  217 us (55%)
  Pallas kernels  69.8 us (18%)
  blocking collectives  51.5 us (13%)
  local copies, waits for them, and re-layouts  37.2 us (9%)
  other arithmetic  11.1 us (3%)
  starting transfers between devices  11 us (3%)
    all_to_all x2, waiting for transfers between devices, exchange(): return lax.all_to_all(x, 'seq', 0, 0, tiled=True)  217 us
    all_to_all x1, blocking collectives, exchange(): return lax.all_to_all(x, 'seq', 0, 0, tiled=True)  51.5 us
    pallas_call x1, Pallas kernels, split_heads(): pl.pallas_call(functools.partial(attention_kernel, 1.0 / HD ** 0.5), out_...  36.4 us
    pallas_call x1, Pallas kernels, split_heads(): pl.pallas_call(functools.partial(hyena_kernel, group_w), out_shape=shape,...  33.3 us
    unnamed x22, local copies, waits for them, and re-layouts  13.6 us
    all_to_all x2, starting transfers between devices, exchange(): return lax.all_to_all(x, 'seq', 0, 0, tiled=True)  11 us
  transfers between devices with their start and end apart: 2, of which 2 were waited for; matrix products, arithmetic and copies ran while one was open for 7% of the time, Pallas kernels for 8%

profile of v1, /device:TPU:0, one launch (start us, length us, event | category | flops | bytes accessed | tf_op | source)
XLA Modules:
  0.0 398.1 jit_solution(11908807882496759806)
XLA Ops:
  0.0 0.0 copy-start
  0.0 6.5 %copy.34 = f32[128,3,4096]{0,2,1:T(8,128)} copy(f32[128,3,4096]{2,0,1:T(8,128)} %param.10) | data formatting | bytes 12582912 | tf_op args[0]
  6.5 6.6 %copy.35 = f32[128,3,32,128]{3,0,1,2:T(8,128)} copy(f32[128,3,32,128]{0,3,2,1:T(8,128)} %bitcast.30) | data formatting | bytes 12582912 | tf_op jit(solution)/shard_map/streams_to_channels/reshape | solution.py:161
  13.1 7.4 %all-to-all-start.1 = ((f32[32,3,128,128]{3,2,1,0:T(8,128)}), f32[32,3,128,128]{3,2,1,0:T(8,128)}, u32[]{:S(2)}, u32[]{:S(2)}) async-start(f32[32,3,128,128]{3,2,1,0:T(8,128)} %bitcast.29), calls=%async_computation.1 | async-start | bytes 12582912 | tf_op jit(solution)/shard_map/streams_to_channels/all_to_all | solution.py:158
  20.5 1.9 copy.28
  22.5 1.9 copy.31
  24.3 1.9 copy.29
  26.2 1.8 copy.32
  28.1 1.9 copy.30
  30.0 1.8 copy.33
  31.8 6.3 %maximum_bitcast_fusion = f32[32,3,128,128]{3,2,1,0:T(8,128)} fusion(f32[1,128,32,128]{3,1,0,2:T(8,128)} %copy.33, f32[1,128,32,128]{3,1,0,2:T(8,128)} %copy.32, f32[1,128,32,128]{3,1,0,2:T(8,128)} %copy.31), kind=kLoop, calls=%fused_computation | loop fusion | flops 3145728 | bytes 12582912 | tf_op jit(solution)/shard_map/qkv_to_heads/transpose | solution.py:165
  38.1 0.0 copy-start.7
  38.1 0.0 copy-start.5
  38.1 122.5 %all-to-all-done.1.s_ref = f32[32,3,128,128]{3,2,1,0:T(8,128)} async-done(((f32[32,3,128,128]{3,2,1,0:T(8,128)}), f32[32,3,128,128]{3,2,1,0:T(8,128)}, u32[]{:S(2)}, u32[]{:S(2)}) %all-to-all-start.1) | async-done | bytes 6291488 | tf_op jit(solution)/shard_map/streams_to_channels/all_to_all | solution.py:158
  160.6 3.6 all-to-all-start
  164.2 0.0 copy-done.7
  164.2 0.1 dynamic-slice_negate_fusion
  164.3 0.0 copy-done.5
  164.3 0.1 multiply_bitcast_fusion
  164.5 0.1 pad.3.clone
  164.5 0.1 maximum_maximum_fusion
  164.6 0.1 tile.4
  164.8 0.1 slice.27
  164.9 0.0 copy-start.4
  164.9 1.7 reshape.89
  166.6 1.1 slice.28
  167.7 0.0 copy-done
  167.7 0.1 constant_dynamic-slice_fusion
  167.8 0.1 broadcast_in_dim.38
  167.9 0.1 reshape.88
  168.0 0.6 copy.38.short_ref
  168.6 0.0 copy-done.4
  168.6 0.1 slice_compare_fusion
  168.6 0.1 add_select_fusion
  168.7 0.3 reduce-window.9
  169.0 0.1 slice.25
  169.1 0.1 reduce-window.12
  169.1 0.1 slice_reduce_fusion
  169.3 0.1 broadcast_maximum_fusion
  169.3 0.0 copy-start.8
  169.3 0.7 copy.37.starts_ref
  170.0 0.0 copy-start.2
  170.0 3.0 broadcast_in_dim.41.docs_ref
  173.0 0.0 copy-done.8
  173.0 0.7 select_reduce_fusion.inv_ref
  173.7 0.7 fusion.1.start_ref
  174.4 1.5 iota_subtract_fusion.place_ref
  175.8 0.0 copy-done.2
  175.8 33.3 %hyena.1.hyena_ref = f32[32,128,128]{2,1,0:T(8,128)} custom-call(s32[32]{0:T(128)} %select_reduce_fusion.inv_ref, s32[4096]{0:T(1024)} %doc_ref.1, f32[32,3,128,128]{3,2,1,0:T(8,128)} %all-to-all-done.1.s_ref, f32[7,3,128]{2,1,0:T(4,128)} %copy.38.short_ref, f32[1024,256]{1,0:T(8,128)} %bitcast.36, s32[4224,1]{1,0:T(8,128)} %broadcast_in_dim.41.docs_ref, ...), custom_call_target="tpu_custom_call" | custom-call | flops 8053063680 | bytes 12582912 | tf_op jit(solution)/shard_map/hyena/pallas_call | solution.py:191
  209.2 95.0 %all-to-all-done.x_ref = f32[32,3,128,128]{3,2,1,0:T(8,128)} async-done(((f32[32,3,128,128]{3,2,1,0:T(8,128)}), f32[32,3,128,128]{3,2,1,0:T(8,128)}, u32[]{:S(2)}, u32[]{:S(2)}) %all-to-all-start) | async-done | bytes 6291488 | tf_op jit(solution)/shard_map/qkv_to_heads/all_to_all | solution.py:158
  304.1 36.4 %attention.1 = f32[32,128,128]{2,1,0:T(8,128)} custom-call(s32[32]{0:T(128)} %select_reduce_fusion.inv_ref, s32[4096]{0:T(1024)} %fusion.1.start_ref, f32[32,3,128,128]{3,2,1,0:T(8,128)} %all-to-all-done.x_ref, f32[32,128,128]{2,1,0:T(8,128)} %hyena.1.hyena_ref, s32[4096,1]{1,0:T(8,128)} %copy-done.2), custom_call_target="tpu_custom_call" | custom-call | flops 6442450944 | bytes 12582912 | tf_op jit(solution)/shard_map/attention/pallas_call | solution.py:211
  340.6 51.5 %all_to_all.15 = f32[32,128,128]{2,1,0:T(8,128)S(1)} all-to-all(f32[32,128,128]{2,1,0:T(8,128)} %attention.1), channel_id=1, replica_groups=mesh['seq'=32,'mp'=1] {'seq'}, dimensions={0} | all-to-all | bytes 4194304 | tf_op jit(solution)/shard_map/back_to_tokens/all_to_all | solution.py:158
  392.1 0.0 copy-start.6
  392.1 1.8 copy.41
  393.9 0.0 copy-start.3
  393.9 0.2 multiply_reduce_fusion
  394.1 0.0 copy-done.6
  394.1 1.3 copy-done.3
  395.5 0.0 copy-start.1
  395.5 0.8 fusion
  396.3 1.8 copy.42
  398.1 0.0 copy-done.1
  (6 shorter events, 0.1 us)
Async XLA Ops:
  0.0 167.7 %copy-start = (f32[7,3,256]{2,0,1:T(8,128)S(1)}, f32[7,3,256]{2,0,1:T(8,128)}, u32[]{:S(2)}) copy-start(f32[7,3,256]{2,0,1:T(8,128)} %param.11) | copy-start | bytes 64516
  13.1 147.4 %all-to-all-start.1 = ((f32[32,3,128,128]{3,2,1,0:T(8,128)}), f32[32,3,128,128]{3,2,1,0:T(8,128)}, u32[]{:S(2)}, u32[]{:S(2)}) async-start(f32[32,3,128,128]{3,2,1,0:T(8,128)} %bitcast.29), calls=%async_computation.1 | async-start | bytes 12582912 | tf_op jit(solution)/shard_map/streams_to_channels/all_to_all | solution.py:158
  38.1 126.1 %copy-start.7 = (f32[256]{0:T(256)S(1)}, f32[256]{0:T(256)}, u32[]{:S(2)}) copy-start(f32[256]{0:T(256)} %param.13) | copy-start | bytes 3076
  38.1 126.2 %copy-start.5 = (f32[128,256]{1,0:T(8,128)S(1)}, f32[128,256]{1,0:T(8,128)}, u32[]{:S(2)}) copy-start(f32[128,256]{1,0:T(8,128)} %param.12) | copy-start | bytes 393220
  160.6 143.6 %all-to-all-start = ((f32[32,3,128,128]{3,2,1,0:T(8,128)}), f32[32,3,128,128]{3,2,1,0:T(8,128)}, u32[]{:S(2)}, u32[]{:S(2)}) async-start(f32[32,3,128,128]{3,2,1,0:T(8,128)} %maximum_bitcast_fusion), calls=%async_computation | async-start | bytes 12582912 | tf_op jit(solution)/shard_map/qkv_to_heads/all_to_all | solution.py:158
  164.9 3.7 copy-start.4
  169.3 3.7 copy-start.8
  170.0 5.9 %copy-start.2 = (s32[4096,1]{1,0:T(8,128)}, s32[4096,1]{1,0:T(8,128)S(1)}, u32[]{:S(2)}) copy-start(s32[4096,1]{1,0:T(8,128)S(1)} %copy.37.starts_ref) | copy-start | bytes 49156
  392.1 2.1 copy-start.6
  393.9 1.6 copy-start.3
  395.5 2.7 copy-start.1

commit v2 on v1

--- a/solution.py
+++ b/solution.py
@@ -21,34 +21,19 @@
     return jnp.dot(a, b, preferred_element_type=jnp.float32)
 
 
-def hyena_kernel(
-    group_w, inv_ref, doc_ref, s_ref, short_ref, long_ref, docs_ref, place_ref, out_ref,
-    ext, window, long_hi, long_lo,
+def conv_kernel(
+    group_w, inv_ref, doc_ref, gated_ref, long_ref, docs_ref, out_ref, window, long_hi, long_lo
 ):
-    count, streams, tok, width = s_ref.shape
-    lags = short_ref.shape[0]
+    count, tok, width = gated_ref.shape
     groups = width // group_w
-    lead = ext.shape[1] - tok
     long_hi[...], long_lo[...] = halves(long_ref[...])
-    ext[...] = jnp.zeros_like(ext)
     window[...] = jnp.zeros_like(window)
     lane_group = lax.broadcasted_iota(jnp.int32, (tok, width), 1) // group_w
 
     def stretch(c, carry):
         b = inv_ref[c]
-        place = place_ref[pl.ds(pl.multiple_of(c * tok, tok), tok), :]
-        for j in range(streams):
-            ext[j, :lead] = ext[j, tok:]
-            ext[j, lead:] = s_ref[b, j]
-        featured = []
-        for j in range(streams):
-            total = short_ref[0, j][None, :] * ext[j, lead:]
-            for lag in range(1, lags):
-                term = short_ref[lag, j][None, :] * ext[j, lead - lag : lead - lag + tok]
-                total = total + jnp.where(place >= lag, term, 0.0)
-            featured.append(total)
         window[:tok] = window[tok:]
-        window[tok:] = featured[1] * featured[2]
+        window[tok:] = gated_ref[b]
         docs = docs_ref[pl.ds(pl.multiple_of(c * tok, tok), 2 * tok), :]
 
         def document(d, conv):
@@ -60,20 +45,19 @@
                 part = jnp.where(lane_group == g, full[g * tok : (g + 1) * tok], part)
             return jnp.where(docs[tok:] == d, part, conv)
 
-        conv = lax.fori_loop(
+        out_ref[b] = lax.fori_loop(
             doc_ref[c * tok],
             doc_ref[c * tok + tok - 1] + 1,
             document,
             jnp.zeros((tok, width), jnp.float32),
         )
-        out_ref[b] = featured[0] * conv
         return carry
 
     lax.fori_loop(0, count, stretch, 0)
 
 
 def attention_kernel(
-    scale, inv_ref, start_ref, x_ref, hyena_ref, starts_ref, out_ref, keys, values
+    scale, inv_ref, start_ref, x_ref, starts_ref, out_ref, keys, values
 ):
     count, _, tok, width = x_ref.shape
     per = TILE // tok
@@ -127,7 +111,7 @@
         )
         attended = acc / total
         for r, b in enumerate(stored):
-            out_ref[b] = attended[r * tok : (r + 1) * tok] + hyena_ref[b]
+            out_ref[b] = attended[r * tok : (r + 1) * tok]
         return carry
 
     lax.fori_loop(0, count // per, rows_of, 0)
@@ -157,16 +141,34 @@
     def exchange(x):
         return lax.all_to_all(x, "seq", 0, 0, tiled=True)
 
-    with jax.named_scope("streams_to_channels"):
-        sent = streams.reshape(tok, kinds, count, width).transpose(2, 1, 0, 3)
-        by_channel = exchange(sent)
+    def to_tokens(x):
+        return exchange(x).transpose(1, 0, 2).reshape(-1, chl)
+
+    reach = se_len - 1
+    stretch = placement_list[me]
+    with jax.named_scope("tails_to_next_stretch"):
+        tails = streams[tok - reach :].reshape(reach * kinds, count, width)
+        tails = exchange(tails.transpose(1, 0, 2))
+        before = placement_list[:, None] - 1 == placement_list[None, :]
+        source = jnp.sum(jnp.where(before, index[None, :], 0), axis=1)
+        tail = to_tokens(tails[source]).reshape(reach, kinds, chl)
     with jax.named_scope("qkv_to_heads"):
         stacked = jnp.stack([query, key, value], axis=0).reshape(3, tok, count, width)
-        by_head = exchange(stacked.transpose(2, 0, 1, 3))
+        stacked, tail = lax.optimization_barrier((stacked.transpose(2, 0, 1, 3), tail))
+        by_head = exchange(stacked)
+    with jax.named_scope("featured"):
+        place = lax.dynamic_slice_in_dim(positions - starts, stretch * tok, tok)
+        extended = jnp.concatenate([tail, streams], axis=0)
+        short = jnp.repeat(se_filter, group_w, axis=2)
+        featured = short[0][None] * streams
+        for lag in range(1, se_len):
+            term = short[lag][None] * extended[reach - lag : reach - lag + tok]
+            featured = featured + jnp.where((place >= lag)[:, None, None], term, 0.0)
+        gated = featured[:, 1] * featured[:, 2]
+    with jax.named_scope("gated_to_channels"):
+        by_channel = exchange(gated.reshape(tok, count, width).transpose(1, 0, 2))
 
     with jax.named_scope("filters"):
-        short = lax.dynamic_slice_in_dim(se_filter, me * groups, groups, 2)
-        short = jnp.repeat(short, group_w, axis=2)
         decays = jnp.arange(mr_len, dtype=jnp.float32)[:, None]
         taps = lax.dynamic_slice_in_dim(mr_filter, me * groups, groups, 1)
         decay = lax.dynamic_slice_in_dim(mr_decay, me * groups, groups, 0)
@@ -188,30 +190,10 @@
     vmem = pl.BlockSpec(memory_space=pltpu.VMEM)
     shape = jax.ShapeDtypeStruct((count, tok, width), jnp.float32)
     params = pltpu.CompilerParams(vmem_limit_bytes=56 * 2**20)
-    hyena = pl.pallas_call(
-        functools.partial(hyena_kernel, group_w),
-        out_shape=shape,
-        in_specs=[smem, smem, vmem, vmem, vmem, vmem, vmem],
-        out_specs=vmem,
-        scratch_shapes=[
-            pltpu.VMEM((kinds, tok + 8, width), jnp.float32),
-            pltpu.VMEM((2 * tok, width), jnp.float32),
-            pltpu.VMEM((groups * tok, 2 * tok), jnp.bfloat16),
-            pltpu.VMEM((groups * tok, 2 * tok), jnp.bfloat16),
-        ],
-        compiler_params=params,
-        cost_estimate=pl.CostEstimate(
-            flops=40 * 6 * groups * tok * 2 * tok * width, bytes_accessed=12 * 2**20,
-            transcendentals=0,
-        ),
-        name="hyena",
-    )(
-        inverse, doc_ids, by_channel, short, long, docs[:, None], (positions - starts)[:, None]
-    )
-    summed = pl.pallas_call(
+    attended = pl.pallas_call(
         functools.partial(attention_kernel, 1.0 / HD**0.5),
         out_shape=shape,
-        in_specs=[smem, smem, vmem, vmem, vmem],
+        in_specs=[smem, smem, vmem, vmem],
         out_specs=vmem,
         scratch_shapes=[
             pltpu.VMEM((tokens, 2 * width), jnp.bfloat16),
@@ -219,14 +201,31 @@
         ],
         compiler_params=params,
         cost_estimate=pl.CostEstimate(
-            flops=12 * tokens * 1024 * width, bytes_accessed=12 * 2**20,
+            flops=40 * tokens * 1024 * width, bytes_accessed=12 * 2**20,
             transcendentals=tokens * 1024,
         ),
         name="attention",
-    )(inverse, starts, by_head, hyena, starts[:, None])
+    )(inverse, starts, by_head, starts[:, None])
+    conv = pl.pallas_call(
+        functools.partial(conv_kernel, group_w),
+        out_shape=shape,
+        in_specs=[smem, smem, vmem, vmem, vmem],
+        out_specs=vmem,
+        scratch_shapes=[
+            pltpu.VMEM((2 * tok, width), jnp.float32),
+            pltpu.VMEM((groups * tok, 2 * tok), jnp.bfloat16),
+            pltpu.VMEM((groups * tok, 2 * tok), jnp.bfloat16),
+        ],
+        compiler_params=params,
+        cost_estimate=pl.CostEstimate(
+            flops=40 * 8 * groups * tok * 2 * tok * width, bytes_accessed=12 * 2**20,
+            transcendentals=0,
+        ),
+        name="conv",
+    )(inverse, doc_ids, by_channel, long, docs[:, None])
     with jax.named_scope("back_to_tokens"):
-        back = exchange(summed)
-        summed = back.transpose(1, 0, 2).reshape(tok, chl)
+        attended = to_tokens(attended)
+        summed = featured[:, 0] * to_tokens(conv) + attended
     row_squares = lax.psum(jnp.sum(summed * summed, axis=1), "mp")
     norm_scale = lax.rsqrt(row_squares / (chl * lax.axis_size("mp")) + 1e-05)
     return summed * norm_scale[:, None] * norm_gain[None, :]

time: 398 us -> 412 us (1.035)
  waiting for transfers between devices: 217 us -> 172 us
  other arithmetic: 11.1 us -> 50 us
  local copies, waits for them, and re-layouts: 37.2 us -> 52 us
  starting transfers between devices: 11 us -> 24 us
  Pallas kernels: 69.8 us -> 59.7 us
    all_to_all x2 -> x5, waiting for transfers between devices: 217 us -> 172 us  [exchange(): return lax.all_to_all(x, 'seq', 0, 0, tiled=True)]
    add x0 -> x1, other arithmetic: none -> 36.2 us  [split_heads(): featured = featured + jnp.where((place >= lag)[:, None, None], term, 0.0)]
    all_to_all x2 -> x5, starting transfers between devices: 11 us -> 24 us  [exchange(): return lax.all_to_all(x, 'seq', 0, 0, tiled=True)]
    pallas_call x1, Pallas kernels: 33.3 us -> 24.8 us  [split_heads(): pl.pallas_call(functools.partial(conv_kernel, group_w), out_shape=shape,...]
    reshape x3, local copies, waits for them, and re-layouts: 7.28 us -> 1.28 us  [the longest x2 1.16 us: split_heads(): tails = streams[tok - reach:].reshape(reach * kinds, count, width)]
    optimization_barrier x0 -> x1, local copies, waits for them, and re-layouts: none -> 4.21 us  [split_heads(): lax.optimization_barrier((stacked.transpose(2, 0, 1, 3), tail))]
    unnamed x22 -> x30, local copies, waits for them, and re-layouts: 13.6 us -> 15.6 us
  transfers between devices with their start and end apart: 2 -> 5, of which waited for: 2 -> 4; matrix products, arithmetic and copies ran while one was open for 7% -> 10% of each run, Pallas kernels for 8% -> 15%
where the time goes in v2:
time: 412 us; the launch traced here: 411 us
  waiting for transfers between devices  172 us (42%)
  Pallas kernels  59.7 us (14%)
  blocking collectives  52.1 us (13%)
  local copies, waits for them, and re-layouts  52 us (13%)
  other arithmetic  50 us (12%)
  starting transfers between devices  24 us (6%)
    all_to_all x5, waiting for transfers between devices, exchange(): return lax.all_to_all(x, 'seq', 0, 0, tiled=True)  172 us
    all_to_all x1, blocking collectives, exchange(): return lax.all_to_all(x, 'seq', 0, 0, tiled=True)  52.1 us
    add x1, other arithmetic, split_heads(): featured = featured + jnp.where((place >= lag)[:, None, None], term, 0.0)  36.2 us
    pallas_call x1, Pallas kernels, split_heads(): pl.pallas_call(functools.partial(attention_kernel, 1.0 / HD ** 0.5), out_...  35 us
    pallas_call x1, Pallas kernels, split_heads(): pl.pallas_call(functools.partial(conv_kernel, group_w), out_shape=shape,...  24.8 us
    all_to_all x5, starting transfers between devices, exchange(): return lax.all_to_all(x, 'seq', 0, 0, tiled=True)  24 us
    unnamed x30, local copies, waits for them, and re-layouts  15.6 us
  transfers between devices with their start and end apart: 5, of which 4 were waited for; matrix products, arithmetic and copies ran while one was open for 10% of the time, Pallas kernels for 15%

profile of v2, /device:TPU:0, one launch (start us, length us, event | category | flops | bytes accessed | tf_op | source)
XLA Modules:
  0.0 411.0 jit_solution(8593387074240801454)
XLA Ops:
  0.0 1.0 slice.106
  1.0 0.2 copy.39
  1.2 0.2 reshape.132
  1.5 0.9 copy.67
  2.4 7.3 %all-to-all-start = ((f32[32,18,128]{2,1,0:T(8,128)}), f32[32,18,128]{2,1,0:T(8,128)S(1)}, u32[]{:S(2)}, u32[]{:S(2)}) async-start(f32[32,18,128]{2,1,0:T(8,128)} %bitcast.58), calls=%async_computation | async-start | bytes 786432 | tf_op jit(solution)/shard_map/tails_to_next_stretch/all_to_all | solution.py:142
  9.7 6.6 %copy.32 = f32[128,3,4096]{0,2,1:T(8,128)} copy(f32[128,3,4096]{2,0,1:T(8,128)} %param.10) | data formatting | bytes 12582912 | tf_op args[0]
  16.3 0.7 select_reduce_fusion.1
  17.2 0.3 reduce-window.9
  17.6 1.9 copy.35
  19.5 1.8 copy.38
  21.3 1.9 copy.34
  23.2 1.8 copy.37
  25.1 1.9 copy.33
  27.0 1.8 copy.36
  28.8 0.2 broadcast_in_dim.140
  29.0 0.2 broadcast_in_dim.141
  29.2 0.2 broadcast_in_dim.137
  29.4 0.2 broadcast_in_dim.138
  29.7 0.2 broadcast_in_dim.134
  29.8 0.2 broadcast_in_dim.135
  30.1 0.2 broadcast_in_dim.131
  30.2 0.2 broadcast_in_dim.132
  30.5 0.2 broadcast_in_dim.128
  30.6 0.2 broadcast_in_dim.129
  30.9 0.2 broadcast_in_dim.122
  31.1 0.2 broadcast_in_dim.123
  31.3 0.2 broadcast_in_dim.118
  31.5 0.2 broadcast_in_dim.119
  31.7 0.6 dynamic_slice.12
  32.9 0.1 slice_reduce_fusion
  33.1 1.3 gather_fusion
  34.4 5.8 %all-to-all-start.1 = ((f32[32,18,128]{2,1,0:T(8,128)}), f32[32,18,128]{2,1,0:T(8,128)S(1)}, u32[]{:S(2)}, u32[]{:S(2)}) async-start(f32[32,18,128]{2,1,0:T(8,128)} %gather_fusion), calls=%async_computation.1 | async-start | bytes 786432 | tf_op jit(solution)/shard_map/tails_to_next_stretch/all_to_all | solution.py:142
  40.4 5.5 %maximum_bitcast_fusion = f32[32,3,128,128]{3,2,1,0:T(8,128)} fusion(f32[1,128,32,128]{3,1,0,2:T(8,128)S(1)} %copy-done.1, f32[1,128,32,128]{3,1,0,2:T(8,128)} %copy.37, f32[1,128,32,128]{3,1,0,2:T(8,128)} %copy.36), kind=kLoop, calls=%fused_computation.35 | loop fusion | flops 3145728 | bytes 12582912 | tf_op jit(solution)/shard_map/qkv_to_heads/transpose | solution.py:157
  45.9 7.5 %all-to-all-done.1 = f32[32,18,128]{2,1,0:T(8,128)S(1)} async-done(((f32[32,18,128]{2,1,0:T(8,128)}), f32[32,18,128]{2,1,0:T(8,128)S(1)}, u32[]{:S(2)}, u32[]{:S(2)}) %all-to-all-start.1) | async-done | bytes 294944 | tf_op jit(solution)/shard_map/tails_to_next_stretch/all_to_all | solution.py:142
  53.5 0.1 reshape.133
  53.6 4.2 %copy.42 = f32[6,3,4096]{0,2,1:T(8,128)} copy(f32[6,3,4096]{2,1,0:T(4,128)S(1)} %reshape.133) | data formatting | bytes 589824 | tf_op jit(solution)/shard_map/qkv_to_heads/optimization_barrier | solution.py:157
  57.8 36.2 %fusion.4 = f32[128,3,4096]{0,2,1:T(8,128)S(1)} fusion(f32[6,3,4096]{0,2,1:T(8,128)} %copy.42, f32[128,3,4096]{0,2,1:T(8,128)} %copy.32, f32[3,4096]{1,0:T(4,128)S(1)} %broadcast_in_dim.141, f32[3,4096]{1,0:T(4,128)S(1)} %broadcast_in_dim.138, f32[3,4096]{1,0:T(4,128)S(1)} %broadcast_in_dim.135, f32[3,4096]{1,0:T(4,128)S(1)} %broadcast_in_dim.132, ...), kind=kLoop, calls=%fused_computation.15 | loop fusion | flops 39321600 | bytes 13222656 | tf_op jit(solution)/shard_map/featured/add | solution.py:166
  94.1 2.6 copy-done
  96.7 1.7 fusion.26
  98.4 1.8 copy.44
  100.2 52.1 %all_to_all.30.gated_ref = f32[32,128,128]{2,1,0:T(8,128)} all-to-all(f32[32,128,128]{2,1,0:T(8,128)} %bitcast.63), channel_id=1, replica_groups=mesh['seq'=32,'mp'=1] {'seq'}, dimensions={0} | all-to-all | bytes 4194304 | tf_op jit(solution)/shard_map/gated_to_channels/all_to_all | solution.py:142
  152.3 3.9 all-to-all-start.4
  156.4 0.1 multiply_bitcast_fusion
  156.6 0.1 maximum_maximum_fusion
  156.7 0.1 tile.4
  156.8 0.1 slice.145
  156.9 1.7 reshape.134
  158.6 1.1 slice.146
  159.7 2.9 broadcast_in_dim.145.docs_ref
  162.6 24.8 %conv.1 = f32[32,128,128]{2,1,0:T(8,128)} custom-call(s32[32]{0:T(128)} %get-tuple-element.10.inv_ref, s32[4096]{0:T(1024)} %doc_ref.1, f32[32,128,128]{2,1,0:T(8,128)} %all_to_all.30.gated_ref, f32[1024,256]{1,0:T(8,128)} %bitcast.69, s32[4224,1]{1,0:T(8,128)} %broadcast_in_dim.145.docs_ref), custom_call_target="tpu_custom_call" | custom-call | flops 10737418240 | bytes 12582912 | tf_op jit(solution)/shard_map/conv/pallas_call | solution.py:209
  187.4 108.8 %all-to-all-done.4.x_ref = f32[32,3,128,128]{3,2,1,0:T(8,128)} async-done(((f32[32,3,128,128]{3,2,1,0:T(8,128)}), f32[32,3,128,128]{3,2,1,0:T(8,128)}, u32[]{:S(2)}, u32[]{:S(2)}) %all-to-all-start.4) | async-done | bytes 6291488 | tf_op jit(solution)/shard_map/qkv_to_heads/all_to_all | solution.py:142
  296.1 2.7 all-to-all-start.3
  298.9 2.0 copy.48.starts_ref
  300.9 35.0 %attention.1 = f32[32,128,128]{2,1,0:T(8,128)} custom-call(s32[32]{0:T(128)} %get-tuple-element.10.inv_ref, s32[4096]{0:T(1024)} %copy-done.7, f32[32,3,128,128]{3,2,1,0:T(8,128)} %all-to-all-done.4.x_ref, s32[4096,1]{1,0:T(8,128)} %copy.48.starts_ref), custom_call_target="tpu_custom_call" | custom-call | flops 21474836480 | bytes 12582912 | tf_op jit(solution)/shard_map/attention/pallas_call | solution.py:193
  335.9 11.8 %all-to-all-done.3 = f32[32,128,128]{2,1,0:T(8,128)S(1)} async-done(((f32[32,128,128]{2,1,0:T(8,128)}), f32[32,128,128]{2,1,0:T(8,128)S(1)}, u32[]{:S(2)}, u32[]{:S(2)}) %all-to-all-start.3) | async-done | bytes 2097184 | tf_op jit(solution)/shard_map/back_to_tokens/all_to_all | solution.py:142
  347.7 4.2 %all-to-all-start.5 = ((f32[32,128,128]{2,1,0:T(8,128)}), f32[32,128,128]{2,1,0:T(8,128)}, u32[]{:S(2)}, u32[]{:S(2)}) async-start(f32[32,128,128]{2,1,0:T(8,128)} %attention.1), calls=%async_computation.5 | async-start | bytes 4194304 | tf_op jit(solution)/shard_map/back_to_tokens/all_to_all | solution.py:142
  351.9 2.9 copy.50
  354.8 1.8 copy.47
  356.7 44.1 %all-to-all-done.5 = f32[32,128,128]{2,1,0:T(8,128)} async-done(((f32[32,128,128]{2,1,0:T(8,128)}), f32[32,128,128]{2,1,0:T(8,128)}, u32[]{:S(2)}, u32[]{:S(2)}) %all-to-all-start.5) | async-done | bytes 2097184 | tf_op jit(solution)/shard_map/back_to_tokens/all_to_all | solution.py:142
  400.7 2.9 copy.49
  403.6 2.8 multiply_reduce_fusion
  406.5 0.6 copy-done.3
  407.1 2.1 fusion.24
  409.2 1.8 copy.51
  (46 shorter events, 0.9 us)
Async XLA Ops:
  2.4 30.7 %all-to-all-start = ((f32[32,18,128]{2,1,0:T(8,128)}), f32[32,18,128]{2,1,0:T(8,128)S(1)}, u32[]{:S(2)}, u32[]{:S(2)}) async-start(f32[32,18,128]{2,1,0:T(8,128)} %bitcast.58), calls=%async_computation | async-start | bytes 786432 | tf_op jit(solution)/shard_map/tails_to_next_stretch/all_to_all | solution.py:142
  9.7 6.6 %copy-start.9 = (s32[32]{0:T(128)S(1)}, s32[32]{0:T(128)}, u32[]{:S(2)}) copy-start(s32[32]{0:T(128)} %param.17) | copy-start | bytes 388
  9.7 7.3 %copy-start.4 = (s32[4096]{0:T(1024)S(1)}, s32[4096]{0:T(1024)}, u32[]{:S(2)}) copy-start(s32[4096]{0:T(1024)} %doc_ref.1) | copy-start | bytes 49156
  23.2 5.6 %copy-start.6 = (f32[7,3,256]{2,0,1:T(8,128)S(1)}, f32[7,3,256]{2,0,1:T(8,128)}, u32[]{:S(2)}) copy-start(f32[7,3,256]{2,0,1:T(8,128)} %param.11) | copy-start | bytes 64516
  28.8 11.6 %copy-start.1 = (f32[1,128,32,128]{3,1,0,2:T(8,128)S(1)}, f32[1,128,32,128]{3,1,0,2:T(8,128)}, u32[]{:S(2)}) copy-start(f32[1,128,32,128]{3,1,0,2:T(8,128)} %copy.38) | copy-start | bytes 6291460
  33.1 12.8 %copy-start.7 = (s32[4096]{0:T(1024)}, s32[4096]{0:T(1024)S(1)}, u32[]{:S(2)}) copy-start(s32[4096]{0:T(1024)S(1)} %fusion.28.start_ref) | copy-start | bytes 49156
  34.4 19.0 %all-to-all-start.1 = ((f32[32,18,128]{2,1,0:T(8,128)}), f32[32,18,128]{2,1,0:T(8,128)S(1)}, u32[]{:S(2)}, u32[]{:S(2)}) async-start(f32[32,18,128]{2,1,0:T(8,128)} %gather_fusion), calls=%async_computation.1 | async-start | bytes 786432 | tf_op jit(solution)/shard_map/tails_to_next_stretch/all_to_all | solution.py:142
  94.0 2.7 copy-start
  152.3 3.9 copy-start.10
  152.3 4.0 copy-start.5
  152.3 143.8 %all-to-all-start.4 = ((f32[32,3,128,128]{3,2,1,0:T(8,128)}), f32[32,3,128,128]{3,2,1,0:T(8,128)}, u32[]{:S(2)}, u32[]{:S(2)}) async-start(f32[32,3,128,128]{3,2,1,0:T(8,128)} %maximum_bitcast_fusion), calls=%async_computation.4 | async-start | bytes 12582912 | tf_op jit(solution)/shard_map/qkv_to_heads/all_to_all | solution.py:142
  296.1 51.6 %all-to-all-start.3 = ((f32[32,128,128]{2,1,0:T(8,128)}), f32[32,128,128]{2,1,0:T(8,128)S(1)}, u32[]{:S(2)}, u32[]{:S(2)}) async-start(f32[32,128,128]{2,1,0:T(8,128)} %conv.1), calls=%async_computation.3 | async-start | bytes 4194304 | tf_op jit(solution)/shard_map/back_to_tokens/all_to_all | solution.py:142
  347.7 53.1 %all-to-all-start.5 = ((f32[32,128,128]{2,1,0:T(8,128)}), f32[32,128,128]{2,1,0:T(8,128)}, u32[]{:S(2)}, u32[]{:S(2)}) async-start(f32[32,128,128]{2,1,0:T(8,128)} %attention.1), calls=%async_computation.5 | async-start | bytes 4194304 | tf_op jit(solution)/shard_map/back_to_tokens/all_to_all | solution.py:142
  356.6 49.8 %copy-start.8 = (f32[4096]{0:T(1024)S(1)}, f32[4096]{0:T(1024)}, u32[]{:S(2)}) copy-start(f32[4096]{0:T(1024)} %param.19) | copy-start | bytes 49156
  403.6 2.9 copy-start.2
  403.6 3.5 copy-start.3

commit v3 on v2

--- a/solution.py
+++ b/solution.py
@@ -57,23 +57,23 @@
 
 
 def attention_kernel(
-    scale, inv_ref, start_ref, x_ref, starts_ref, out_ref, keys, values
+    scale, inv_ref, start_ref, q_ref, kv_ref, starts_ref, out_ref, keys, values
 ):
-    count, _, tok, width = x_ref.shape
+    count, tok, width = q_ref.shape
     per = TILE // tok
 
     def prepare(c, carry):
         rows = pl.ds(pl.multiple_of(c * tok, tok), tok)
         b = inv_ref[c]
-        keys[rows, :] = jnp.concatenate(halves(x_ref[b, 1]), axis=1)
-        values[rows, :] = jnp.concatenate(halves(x_ref[b, 2]), axis=1)
+        keys[rows, :] = jnp.concatenate(halves(kv_ref[b, 0]), axis=1)
+        values[rows, :] = jnp.concatenate(halves(kv_ref[b, 1]), axis=1)
         return carry
 
     lax.fori_loop(0, count, prepare, 0)
 
     def rows_of(i, carry):
         stored = [inv_ref[i * per + r] for r in range(per)]
-        q = jnp.concatenate([x_ref[b, 0] for b in stored], axis=0) * scale
+        q = jnp.concatenate([q_ref[b] for b in stored], axis=0) * scale
         q_hi, q_lo = halves(q)
         q_both = jnp.concatenate([q_hi, q_hi], axis=1)
         starts = starts_ref[pl.ds(pl.multiple_of(i * TILE, TILE), TILE), :]
@@ -141,8 +141,8 @@
     def exchange(x):
         return lax.all_to_all(x, "seq", 0, 0, tiled=True)
 
-    def to_tokens(x):
-        return exchange(x).transpose(1, 0, 2).reshape(-1, chl)
+    def as_tokens(x):
+        return x.transpose(1, 0, 2).reshape(-1, chl)
 
     reach = se_len - 1
     stretch = placement_list[me]
@@ -151,11 +151,17 @@
         tails = exchange(tails.transpose(1, 0, 2))
         before = placement_list[:, None] - 1 == placement_list[None, :]
         source = jnp.sum(jnp.where(before, index[None, :], 0), axis=1)
-        tail = to_tokens(tails[source]).reshape(reach, kinds, chl)
-    with jax.named_scope("qkv_to_heads"):
-        stacked = jnp.stack([query, key, value], axis=0).reshape(3, tok, count, width)
-        stacked, tail = lax.optimization_barrier((stacked.transpose(2, 0, 1, 3), tail))
-        by_head = exchange(stacked)
+        tail = as_tokens(exchange(tails[source])).reshape(reach, kinds, chl)
+    def by_block(x):
+        return x.reshape(tok, count, width).transpose(1, 0, 2)
+
+    with jax.named_scope("query_to_heads"):
+        sent, tail = lax.optimization_barrier((by_block(query), tail))
+        q_head = exchange(sent)
+    with jax.named_scope("key_value_to_heads"):
+        sent = jnp.stack([by_block(key), by_block(value)], axis=1)
+        sent, q_head, tail = lax.optimization_barrier((sent, q_head, tail))
+        kv_head = exchange(sent)
     with jax.named_scope("featured"):
         place = lax.dynamic_slice_in_dim(positions - starts, stretch * tok, tok)
         extended = jnp.concatenate([tail, streams], axis=0)
@@ -166,7 +172,8 @@
             featured = featured + jnp.where((place >= lag)[:, None, None], term, 0.0)
         gated = featured[:, 1] * featured[:, 2]
     with jax.named_scope("gated_to_channels"):
-        by_channel = exchange(gated.reshape(tok, count, width).transpose(1, 0, 2))
+        sent, kv_head = lax.optimization_barrier((by_block(gated), kv_head))
+        by_channel = exchange(sent)
 
     with jax.named_scope("filters"):
         decays = jnp.arange(mr_len, dtype=jnp.float32)[:, None]
@@ -193,7 +200,7 @@
     attended = pl.pallas_call(
         functools.partial(attention_kernel, 1.0 / HD**0.5),
         out_shape=shape,
-        in_specs=[smem, smem, vmem, vmem],
+        in_specs=[smem, smem, vmem, vmem, vmem],
         out_specs=vmem,
         scratch_shapes=[
             pltpu.VMEM((tokens, 2 * width), jnp.bfloat16),
@@ -205,7 +212,8 @@
             transcendentals=tokens * 1024,
         ),
         name="attention",
-    )(inverse, starts, by_head, starts[:, None])
+    )(inverse, starts, q_head, kv_head, starts[:, None])
+    by_channel, attended = lax.optimization_barrier((by_channel, attended))
     conv = pl.pallas_call(
         functools.partial(conv_kernel, group_w),
         out_shape=shape,
@@ -224,8 +232,8 @@
         name="conv",
     )(inverse, doc_ids, by_channel, long, docs[:, None])
     with jax.named_scope("back_to_tokens"):
-        attended = to_tokens(attended)
-        summed = featured[:, 0] * to_tokens(conv) + attended
+        conv, attended = lax.optimization_barrier((conv, exchange(attended)))
+        summed = featured[:, 0] * as_tokens(exchange(conv)) + as_tokens(attended)
     row_squares = lax.psum(jnp.sum(summed * summed, axis=1), "mp")
     norm_scale = lax.rsqrt(row_squares / (chl * lax.axis_size("mp")) + 1e-05)
     return summed * norm_scale[:, None] * norm_gain[None, :]

time: 412 us -> 362 us (0.88)
  blocking collectives: 52.1 us -> 0 us
  waiting for transfers between devices: 172 us -> 161 us
  starting transfers between devices: 24 us -> 29.7 us
  local copies, waits for them, and re-layouts: 52 us -> 57.2 us
    all_to_all x1 -> x0, blocking collectives: 52.1 us -> none  [exchange(): return lax.all_to_all(x, 'seq', 0, 0, tiled=True)]
    all_to_all x5 -> x7, waiting for transfers between devices: 172 us -> 161 us  [exchange(): return lax.all_to_all(x, 'seq', 0, 0, tiled=True)]
    all_to_all x5 -> x7, starting transfers between devices: 24 us -> 29.7 us  [exchange(): return lax.all_to_all(x, 'seq', 0, 0, tiled=True)]
    transpose x1 -> x0, other arithmetic: 5.55 us -> none  [split_heads(): stacked.transpose(2, 0, 1, 3)]
    reshape x1 -> x4, local copies, waits for them, and re-layouts: 0.12 us -> 5.62 us  [the longest x3 5.5 us: by_block(): return x.reshape(tok, count, width).transpose(1, 0, 2)]
    another operation x4 -> x1, local copies, waits for them, and re-layouts: 5.56 us -> 0.11 us  [the longest x3 5.45 us: split_heads(): jnp.stack([query, key, value], axis=0).reshape(3, tok, count, width)]
    another operation x2 -> x3, other arithmetic: 0.34 us -> 5.01 us  [the longest x1 4.67 us: split_heads(): sent = jnp.stack([by_block(key), by_block(value)], axis=1)]
  transfers between devices with their start and end apart: 5 -> 7, of which waited for: 4 -> 7; matrix products, arithmetic and copies ran while one was open for 10% -> 25% of each run, Pallas kernels for 15% -> 17%
where the time goes in v3:
time: 362 us; the launch traced here: 361 us
  waiting for transfers between devices  161 us (44%)
  Pallas kernels  61.1 us (17%)
  local copies, waits for them, and re-layouts  57.2 us (16%)
  other arithmetic  51 us (14%)
  starting transfers between devices  29.7 us (8%)
    all_to_all x7, waiting for transfers between devices, exchange(): return lax.all_to_all(x, 'seq', 0, 0, tiled=True)  161 us
    add x1, other arithmetic, split_heads(): featured = featured + jnp.where((place >= lag)[:, None, None], term, 0.0)  36.5 us
    pallas_call x1, Pallas kernels, split_heads(): pl.pallas_call(functools.partial(attention_kernel, 1.0 / HD ** 0.5), out_...  36.3 us
    all_to_all x7, starting transfers between devices, exchange(): return lax.all_to_all(x, 'seq', 0, 0, tiled=True)  29.7 us
    pallas_call x1, Pallas kernels, split_heads(): pl.pallas_call(functools.partial(conv_kernel, group_w), out_shape=shape,...  24.8 us
    unnamed x30, local copies, waits for them, and re-layouts  15.7 us
  transfers between devices with their start and end apart: 7, of which 7 were waited for; matrix products, arithmetic and copies ran while one was open for 25% of the time, Pallas kernels for 17%

profile of v3, /device:TPU:0, one launch (start us, length us, event | category | flops | bytes accessed | tf_op | source)
XLA Modules:
  0.0 360.9 jit_solution(11761978580725262314)
XLA Ops:
  0.0 1.0 slice.106
  1.0 0.2 copy.39
  1.2 0.2 reshape.137
  1.5 0.9 copy.67
  2.4 7.3 %all-to-all-start = ((f32[32,18,128]{2,1,0:T(8,128)}), f32[32,18,128]{2,1,0:T(8,128)S(1)}, u32[]{:S(2)}, u32[]{:S(2)}) async-start(f32[32,18,128]{2,1,0:T(8,128)} %bitcast.63), calls=%async_computation | async-start | bytes 786432 | tf_op jit(solution)/shard_map/tails_to_next_stretch/all_to_all | solution.py:142
  9.7 0.7 broadcast_add_fusion
  10.4 1.4 select_reduce_fusion.1
  11.7 11.1 %all-to-all-done = f32[32,18,128]{2,1,0:T(8,128)S(1)} async-done(((f32[32,18,128]{2,1,0:T(8,128)}), f32[32,18,128]{2,1,0:T(8,128)S(1)}, u32[]{:S(2)}, u32[]{:S(2)}) %all-to-all-start) | async-done | bytes 294944 | tf_op jit(solution)/shard_map/tails_to_next_stretch/all_to_all | solution.py:142
  22.9 1.3 gather_fusion
  24.2 2.6 all-to-all-start.1
  26.9 1.9 copy.37
  28.8 1.8 copy.38
  30.6 9.4 %all-to-all-done.1 = f32[32,18,128]{2,1,0:T(8,128)S(1)} async-done(((f32[32,18,128]{2,1,0:T(8,128)}), f32[32,18,128]{2,1,0:T(8,128)S(1)}, u32[]{:S(2)}, u32[]{:S(2)}) %all-to-all-start.1) | async-done | bytes 294944 | tf_op jit(solution)/shard_map/tails_to_next_stretch/all_to_all | solution.py:142
  40.2 3.5 all-to-all-start.2
  43.7 1.9 copy.35
  45.6 1.8 copy.36
  47.5 1.9 copy.33
  49.4 1.8 copy.34
  51.2 4.7 %pad_maximum_fusion.1 = f32[32,2,128,128]{3,2,1,0:T(8,128)} fusion(f32[32,1,128,128]{3,2,1,0:T(8,128)} %bitcast.72, f32[32,1,128,128]{3,2,1,0:T(8,128)} %bitcast.73), kind=kLoop, calls=%fused_computation.35 | loop fusion | flops 1048576 | bytes 8388608 | tf_op jit(solution)/shard_map/key_value_to_heads/stack | solution.py:162
  55.9 36.7 %all-to-all-done.2.q_ref = f32[32,128,128]{2,1,0:T(8,128)} async-done(((f32[32,128,128]{2,1,0:T(8,128)}), f32[32,128,128]{2,1,0:T(8,128)}, u32[]{:S(2)}, u32[]{:S(2)}) %all-to-all-start.2) | async-done | bytes 2097184 | tf_op jit(solution)/shard_map/query_to_heads/all_to_all | solution.py:142
  92.6 4.0 %all-to-all-start.3 = ((f32[32,2,128,128]{3,2,1,0:T(8,128)}), f32[32,2,128,128]{3,2,1,0:T(8,128)}, u32[]{:S(2)}, u32[]{:S(2)}) async-start(f32[32,2,128,128]{3,2,1,0:T(8,128)} %pad_maximum_fusion.1), calls=%async_computation.3 | async-start | bytes 8388608 | tf_op jit(solution)/shard_map/key_value_to_heads/all_to_all | solution.py:142
  96.7 6.5 %copy.32 = f32[128,3,4096]{0,2,1:T(8,128)} copy(f32[128,3,4096]{2,0,1:T(8,128)} %param.10) | data formatting | bytes 12582912 | tf_op args[0]
  103.2 0.2 broadcast_in_dim.140
  103.4 0.2 broadcast_in_dim.141
  103.6 0.2 broadcast_in_dim.137
  103.8 0.2 broadcast_in_dim.138
  104.1 0.2 broadcast_in_dim.134
  104.2 0.2 broadcast_in_dim.135
  104.5 0.2 broadcast_in_dim.131
  104.6 0.2 broadcast_in_dim.132
  104.9 0.2 broadcast_in_dim.128
  105.0 0.2 broadcast_in_dim.129
  105.3 0.2 broadcast_in_dim.122
  105.5 0.2 broadcast_in_dim.123
  105.9 0.2 broadcast_in_dim.119
  106.3 0.3 reduce-window.9
  106.7 0.6 dynamic_slice.12
  108.2 4.2 %copy.42 = f32[6,3,4096]{0,2,1:T(8,128)} copy(f32[6,3,4096]{2,1,0:T(4,128)S(1)} %reshape.138) | data formatting | bytes 589824 | tf_op jit(solution)/shard_map/key_value_to_heads/optimization_barrier | solution.py:163
  112.4 36.5 %fusion.4 = f32[128,3,4096]{0,2,1:T(8,128)S(1)} fusion(f32[6,3,4096]{0,2,1:T(8,128)} %copy.42, f32[128,3,4096]{0,2,1:T(8,128)} %copy.32, f32[3,4096]{1,0:T(4,128)S(1)} %broadcast_in_dim.141, f32[3,4096]{1,0:T(4,128)S(1)} %broadcast_in_dim.138, f32[3,4096]{1,0:T(4,128)S(1)} %broadcast_in_dim.135, f32[3,4096]{1,0:T(4,128)S(1)} %broadcast_in_dim.132, ...), kind=kLoop, calls=%fused_computation.15 | loop fusion | flops 39321600 | bytes 13222656 | tf_op jit(solution)/shard_map/featured/add | solution.py:172
  148.9 2.0 fusion.26
  150.9 1.5 copy-done
  152.3 1.9 copy.44
  154.2 36.3 %all-to-all-done.3.kv_ref = f32[32,2,128,128]{3,2,1,0:T(8,128)} async-done(((f32[32,2,128,128]{3,2,1,0:T(8,128)}), f32[32,2,128,128]{3,2,1,0:T(8,128)}, u32[]{:S(2)}, u32[]{:S(2)}) %all-to-all-start.3) | async-done | bytes 4194336 | tf_op jit(solution)/shard_map/key_value_to_heads/all_to_all | solution.py:142
  190.5 4.0 %all-to-all-start.4 = ((f32[32,128,128]{2,1,0:T(8,128)}), f32[32,128,128]{2,1,0:T(8,128)S(1)}, u32[]{:S(2)}, u32[]{:S(2)}) async-start(f32[32,128,128]{2,1,0:T(8,128)} %bitcast.68), calls=%async_computation.4 | async-start | bytes 4194304 | tf_op jit(solution)/shard_map/gated_to_channels/all_to_all | solution.py:142
  194.6 2.0 copy.45.starts_ref
  196.5 36.3 %attention.1 = f32[32,128,128]{2,1,0:T(8,128)} custom-call(s32[32]{0:T(128)} %get-tuple-element.28.inv_ref, s32[4096]{0:T(1024)} %copy-done.7, f32[32,128,128]{2,1,0:T(8,128)} %all-to-all-done.2.q_ref, f32[32,2,128,128]{3,2,1,0:T(8,128)} %all-to-all-done.3.kv_ref, s32[4096,1]{1,0:T(8,128)} %copy.45.starts_ref), custom_call_target="tpu_custom_call" | custom-call | flops 21474836480 | bytes 12582912 | tf_op jit(solution)/shard_map/attention/pallas_call | solution.py:200
  232.8 10.6 %all-to-all-done.4.gated_ref = f32[32,128,128]{2,1,0:T(8,128)S(1)} async-done(((f32[32,128,128]{2,1,0:T(8,128)}), f32[32,128,128]{2,1,0:T(8,128)S(1)}, u32[]{:S(2)}, u32[]{:S(2)}) %all-to-all-start.4) | async-done | bytes 2097184 | tf_op jit(solution)/shard_map/gated_to_channels/all_to_all | solution.py:142
  243.4 1.3 copy-done.3
  244.7 4.2 %all-to-all-start.5 = ((f32[32,128,128]{2,1,0:T(8,128)}), f32[32,128,128]{2,1,0:T(8,128)S(1)}, u32[]{:S(2)}, u32[]{:S(2)}) async-start(f32[32,128,128]{2,1,0:T(8,128)} %attention.1), calls=%async_computation.5 | async-start | bytes 4194304 | tf_op jit(solution)/shard_map/back_to_tokens/all_to_all | solution.py:142
  249.5 1.2 slice.145
  250.7 4.2 %reshape.139 = f32[8,128,383]{2,1,0:T(8,128)} reshape(f32[8,49024]{1,0:T(8,128)} %slice.145) | data formatting | bytes 3137536 | tf_op jit(solution)/shard_map/filters/reshape | solution.py:193
  254.9 2.3 slice.146
  257.2 3.0 broadcast_in_dim.145.docs_ref
  260.3 24.8 %conv.1 = f32[32,128,128]{2,1,0:T(8,128)} custom-call(s32[32]{0:T(128)} %get-tuple-element.28.inv_ref, s32[4096]{0:T(1024)} %doc_ref.1, f32[32,128,128]{2,1,0:T(8,128)} %copy-done.3, f32[1024,256]{1,0:T(8,128)} %bitcast.76, s32[4224,1]{1,0:T(8,128)} %broadcast_in_dim.145.docs_ref), custom_call_target="tpu_custom_call" | custom-call | flops 10737418240 | bytes 12582912 | tf_op jit(solution)/shard_map/conv/pallas_call | solution.py:217
  285.0 12.6 %all-to-all-done.5 = f32[32,128,128]{2,1,0:T(8,128)S(1)} async-done(((f32[32,128,128]{2,1,0:T(8,128)}), f32[32,128,128]{2,1,0:T(8,128)S(1)}, u32[]{:S(2)}, u32[]{:S(2)}) %all-to-all-start.5) | async-done | bytes 2097184 | tf_op jit(solution)/shard_map/back_to_tokens/all_to_all | solution.py:142
  297.7 4.1 %all-to-all-start.6 = ((f32[32,128,128]{2,1,0:T(8,128)}), f32[32,128,128]{2,1,0:T(8,128)}, u32[]{:S(2)}, u32[]{:S(2)}) async-start(f32[32,128,128]{2,1,0:T(8,128)} %conv.1), calls=%async_computation.6 | async-start | bytes 4194304 | tf_op jit(solution)/shard_map/back_to_tokens/all_to_all | solution.py:142
  301.8 2.9 copy.50
  304.7 1.8 copy.49
  306.5 44.1 %all-to-all-done.6 = f32[32,128,128]{2,1,0:T(8,128)} async-done(((f32[32,128,128]{2,1,0:T(8,128)}), f32[32,128,128]{2,1,0:T(8,128)}, u32[]{:S(2)}, u32[]{:S(2)}) %all-to-all-start.6) | async-done | bytes 2097184 | tf_op jit(solution)/shard_map/back_to_tokens/all_to_all | solution.py:142
  350.6 2.9 copy.48
  353.6 2.8 multiply_reduce_fusion
  356.4 0.6 copy-done.2
  357.1 2.1 fusion.24
  359.1 1.8 copy.51
  (49 shorter events, 1.6 us)
Async XLA Ops:
  2.4 20.5 %all-to-all-start = ((f32[32,18,128]{2,1,0:T(8,128)}), f32[32,18,128]{2,1,0:T(8,128)S(1)}, u32[]{:S(2)}, u32[]{:S(2)}) async-start(f32[32,18,128]{2,1,0:T(8,128)} %bitcast.63), calls=%async_computation | async-start | bytes 786432 | tf_op jit(solution)/shard_map/tails_to_next_stretch/all_to_all | solution.py:142
  24.2 15.8 %all-to-all-start.1 = ((f32[32,18,128]{2,1,0:T(8,128)}), f32[32,18,128]{2,1,0:T(8,128)S(1)}, u32[]{:S(2)}, u32[]{:S(2)}) async-start(f32[32,18,128]{2,1,0:T(8,128)} %gather_fusion), calls=%async_computation.1 | async-start | bytes 786432 | tf_op jit(solution)/shard_map/tails_to_next_stretch/all_to_all | solution.py:142
  40.2 52.4 %all-to-all-start.2 = ((f32[32,128,128]{2,1,0:T(8,128)}), f32[32,128,128]{2,1,0:T(8,128)}, u32[]{:S(2)}, u32[]{:S(2)}) async-start(f32[32,128,128]{2,1,0:T(8,128)} %bitcast.10), calls=%async_computation.2 | async-start | bytes 4194304 | tf_op jit(solution)/shard_map/query_to_heads/all_to_all | solution.py:142
  92.6 97.9 %all-to-all-start.3 = ((f32[32,2,128,128]{3,2,1,0:T(8,128)}), f32[32,2,128,128]{3,2,1,0:T(8,128)}, u32[]{:S(2)}, u32[]{:S(2)}) async-start(f32[32,2,128,128]{3,2,1,0:T(8,128)} %pad_maximum_fusion.1), calls=%async_computation.3 | async-start | bytes 8388608 | tf_op jit(solution)/shard_map/key_value_to_heads/all_to_all | solution.py:142
  96.6 6.5 %copy-start.6 = (f32[7,3,256]{2,0,1:T(8,128)S(1)}, f32[7,3,256]{2,0,1:T(8,128)}, u32[]{:S(2)}) copy-start(f32[7,3,256]{2,0,1:T(8,128)} %param.11) | copy-start | bytes 64516
  103.2 2.9 copy-start.4
  103.2 3.5 copy-start.9
  108.1 40.8 %copy-start.7 = (s32[4096]{0:T(1024)}, s32[4096]{0:T(1024)S(1)}, u32[]{:S(2)}) copy-start(s32[4096]{0:T(1024)S(1)} %fusion.28.start_ref) | copy-start | bytes 49156
  148.9 3.4 copy-start
  190.5 52.9 %all-to-all-start.4 = ((f32[32,128,128]{2,1,0:T(8,128)}), f32[32,128,128]{2,1,0:T(8,128)S(1)}, u32[]{:S(2)}, u32[]{:S(2)}) async-start(f32[32,128,128]{2,1,0:T(8,128)} %bitcast.68), calls=%async_computation.4 | async-start | bytes 4194304 | tf_op jit(solution)/shard_map/gated_to_channels/all_to_all | solution.py:142
  232.8 16.1 %copy-start.10 = (f32[256]{0:T(256)S(1)}, f32[256]{0:T(256)}, u32[]{:S(2)}) copy-start(f32[256]{0:T(256)} %param.13) | copy-start | bytes 3076
  232.8 16.2 %copy-start.5 = (f32[128,256]{1,0:T(8,128)S(1)}, f32[128,256]{1,0:T(8,128)}, u32[]{:S(2)}) copy-start(f32[128,256]{1,0:T(8,128)} %param.12) | copy-start | bytes 393220
  243.4 1.3 copy-start.3
  244.7 53.0 %all-to-all-start.5 = ((f32[32,128,128]{2,1,0:T(8,128)}), f32[32,128,128]{2,1,0:T(8,128)S(1)}, u32[]{:S(2)}, u32[]{:S(2)}) async-start(f32[32,128,128]{2,1,0:T(8,128)} %attention.1), calls=%async_computation.5 | async-start | bytes 4194304 | tf_op jit(solution)/shard_map/back_to_tokens/all_to_all | solution.py:142
  297.7 53.0 %all-to-all-start.6 = ((f32[32,128,128]{2,1,0:T(8,128)}), f32[32,128,128]{2,1,0:T(8,128)}, u32[]{:S(2)}, u32[]{:S(2)}) async-start(f32[32,128,128]{2,1,0:T(8,128)} %conv.1), calls=%async_computation.6 | async-start | bytes 4194304 | tf_op jit(solution)/shard_map/back_to_tokens/all_to_all | solution.py:142
  353.6 2.9 copy-start.1
  353.6 3.5 copy-start.2
  353.6 3.5 copy-start.8

commit v4 on v3

--- a/solution.py
+++ b/solution.py
@@ -22,9 +22,13 @@
 
 
 def conv_kernel(
-    group_w, inv_ref, doc_ref, gated_ref, long_ref, docs_ref, out_ref, window, long_hi, long_lo
+    group_w, inv_ref, doc_ref, packed_ref, short_ref, long_ref, docs_ref, place_ref, out_ref,
+    ext, window, long_hi, long_lo,
 ):
-    count, tok, width = gated_ref.shape
+    count, tok, width = out_ref.shape
+    lags, kinds, _ = short_ref.shape
+    lead = ext.shape[1] // 2
+    inner = tok - lead
     groups = width // group_w
     long_hi[...], long_lo[...] = halves(long_ref[...])
     window[...] = jnp.zeros_like(window)
@@ -32,8 +36,21 @@
 
     def stretch(c, carry):
         b = inv_ref[c]
+        before = inv_ref[jnp.maximum(c - 1, 0)]
+        place = place_ref[pl.ds(pl.multiple_of(c * tok, tok), lead), :]
+        edge = []
+        for j in range(kinds):
+            tail, first = inner + j * lead, inner + (kinds + j) * lead
+            ext[j, :lead] = packed_ref[before, tail : tail + lead]
+            ext[j, lead:] = packed_ref[b, first : first + lead]
+            total = short_ref[0, j][None, :] * ext[j, lead:]
+            for lag in range(1, lags):
+                term = short_ref[lag, j][None, :] * ext[j, lead - lag : 2 * lead - lag]
+                total = total + jnp.where(place >= lag, term, 0.0)
+            edge.append(total)
         window[:tok] = window[tok:]
-        window[tok:] = gated_ref[b]
+        window[tok : tok + lead] = edge[1] * edge[2]
+        window[tok + lead :] = packed_ref[b, :inner]
         docs = docs_ref[pl.ds(pl.multiple_of(c * tok, tok), 2 * tok), :]
 
         def document(d, conv):
@@ -45,12 +62,14 @@
                 part = jnp.where(lane_group == g, full[g * tok : (g + 1) * tok], part)
             return jnp.where(docs[tok:] == d, part, conv)
 
-        out_ref[b] = lax.fori_loop(
+        conv = lax.fori_loop(
             doc_ref[c * tok],
             doc_ref[c * tok + tok - 1] + 1,
             document,
             jnp.zeros((tok, width), jnp.float32),
         )
+        out_ref[b, :lead] = edge[0] * conv[:lead]
+        out_ref[b, lead:] = conv[lead:]
         return carry
 
     lax.fori_loop(0, count, stretch, 0)
@@ -144,38 +163,37 @@
     def as_tokens(x):
         return x.transpose(1, 0, 2).reshape(-1, chl)
 
-    reach = se_len - 1
+    lead = -(-(se_len - 1) // 8) * 8
     stretch = placement_list[me]
-    with jax.named_scope("tails_to_next_stretch"):
-        tails = streams[tok - reach :].reshape(reach * kinds, count, width)
-        tails = exchange(tails.transpose(1, 0, 2))
-        before = placement_list[:, None] - 1 == placement_list[None, :]
-        source = jnp.sum(jnp.where(before, index[None, :], 0), axis=1)
-        tail = as_tokens(exchange(tails[source])).reshape(reach, kinds, chl)
+    places = positions - starts
+
     def by_block(x):
-        return x.reshape(tok, count, width).transpose(1, 0, 2)
+        return x.reshape(-1, count, width).transpose(1, 0, 2)
 
     with jax.named_scope("query_to_heads"):
-        sent, tail = lax.optimization_barrier((by_block(query), tail))
-        q_head = exchange(sent)
+        q_head = exchange(by_block(query))
     with jax.named_scope("key_value_to_heads"):
+        place = lax.dynamic_slice_in_dim(places, stretch * tok, tok)[lead:]
         sent = jnp.stack([by_block(key), by_block(value)], axis=1)
-        sent, q_head, tail = lax.optimization_barrier((sent, q_head, tail))
+        sent, q_head, place = lax.optimization_barrier((sent, q_head, place))
         kv_head = exchange(sent)
     with jax.named_scope("featured"):
-        place = lax.dynamic_slice_in_dim(positions - starts, stretch * tok, tok)
-        extended = jnp.concatenate([tail, streams], axis=0)
         short = jnp.repeat(se_filter, group_w, axis=2)
-        featured = short[0][None] * streams
+        featured = short[0][None] * streams[lead:]
         for lag in range(1, se_len):
-            term = short[lag][None] * extended[reach - lag : reach - lag + tok]
+            term = short[lag][None] * streams[lead - lag : tok - lag]
             featured = featured + jnp.where((place >= lag)[:, None, None], term, 0.0)
         gated = featured[:, 1] * featured[:, 2]
     with jax.named_scope("gated_to_channels"):
-        sent, kv_head = lax.optimization_barrier((by_block(gated), kv_head))
+        ends = [streams[tok - lead :, j] for j in range(kinds)]
+        ends += [streams[:lead, j] for j in range(kinds)]
+        packed = by_block(jnp.concatenate([gated] + ends, axis=0))
+        sent, kv_head = lax.optimization_barrier((packed, kv_head))
         by_channel = exchange(sent)
 
     with jax.named_scope("filters"):
+        short = lax.dynamic_slice_in_dim(se_filter, me * groups, groups, 2)
+        short = jnp.repeat(short, group_w, axis=2)
         decays = jnp.arange(mr_len, dtype=jnp.float32)[:, None]
         taps = lax.dynamic_slice_in_dim(mr_filter, me * groups, groups, 1)
         decay = lax.dynamic_slice_in_dim(mr_decay, me * groups, groups, 0)
@@ -217,9 +235,10 @@
     conv = pl.pallas_call(
         functools.partial(conv_kernel, group_w),
         out_shape=shape,
-        in_specs=[smem, smem, vmem, vmem, vmem],
+        in_specs=[smem, smem, vmem, vmem, vmem, vmem, vmem],
         out_specs=vmem,
         scratch_shapes=[
+            pltpu.VMEM((kinds, 2 * lead, width), jnp.float32),
             pltpu.VMEM((2 * tok, width), jnp.float32),
             pltpu.VMEM((groups * tok, 2 * tok), jnp.bfloat16),
             pltpu.VMEM((groups * tok, 2 * tok), jnp.bfloat16),
@@ -230,10 +249,11 @@
             transcendentals=0,
         ),
         name="conv",
-    )(inverse, doc_ids, by_channel, long, docs[:, None])
+    )(inverse, doc_ids, by_channel, short, long, docs[:, None], places[:, None])
     with jax.named_scope("back_to_tokens"):
         conv, attended = lax.optimization_barrier((conv, exchange(attended)))
-        summed = featured[:, 0] * as_tokens(exchange(conv)) + as_tokens(attended)
+        outer = jnp.concatenate([jnp.ones((lead, chl), jnp.float32), featured[:, 0]], axis=0)
+        summed = outer * as_tokens(exchange(conv)) + as_tokens(attended)
     row_squares = lax.psum(jnp.sum(summed * summed, axis=1), "mp")
     norm_scale = lax.rsqrt(row_squares / (chl * lax.axis_size("mp")) + 1e-05)
     return summed * norm_scale[:, None] * norm_gain[None, :]

time: 362 us -> 366 us (1.011)
  local copies, waits for them, and re-layouts: 57.2 us -> 130 us
  waiting for transfers between devices: 161 us -> 113 us
  other arithmetic: 51 us -> 32.1 us
  starting transfers between devices: 29.7 us -> 25.8 us
    all_to_all x7 -> x5, waiting for transfers between devices: 161 us -> 113 us  [exchange(): return lax.all_to_all(x, 'seq', 0, 0, tiled=True)]
    unnamed x30 -> x40, local copies, waits for them, and re-layouts: 15.7 us -> 62.6 us
    slice x4, local copies, waits for them, and re-layouts: 1.33 us -> 31 us  [the longest x2 30.9 us: split_heads(): featured = short[0][None] * streams[lead:]]
    add x1, other arithmetic: 36.5 us -> 17.2 us  [split_heads(): featured = featured + jnp.where((place >= lag)[:, None, None], term, 0.0)]
    optimization_barrier x1 -> x0, local copies, waits for them, and re-layouts: 4.2 us -> none  [split_heads(): sent, q_head, tail = lax.optimization_barrier((sent, q_head, tail))]
    all_to_all x7 -> x5, starting transfers between devices: 29.7 us -> 25.8 us  [exchange(): return lax.all_to_all(x, 'seq', 0, 0, tiled=True)]
  transfers between devices with their start and end apart: 7 -> 5, of which waited for: 7 -> 4; matrix products, arithmetic and copies ran while one was open for 25% -> 40% of each run, Pallas kernels for 17% -> 17%
where the time goes in v4:
time: 366 us; the launch traced here: 364 us
  local copies, waits for them, and re-layouts  130 us (36%)
  waiting for transfers between devices  113 us (31%)
  Pallas kernels  62.7 us (17%)
  other arithmetic  32.1 us (9%)
  starting transfers between devices  25.8 us (7%)
    all_to_all x5, waiting for transfers between devices, exchange(): return lax.all_to_all(x, 'seq', 0, 0, tiled=True)  113 us
    unnamed x40, local copies, waits for them, and re-layouts  62.6 us
    pallas_call x1, Pallas kernels, split_heads(): pl.pallas_call(functools.partial(attention_kernel, 1.0 / HD ** 0.5), out_...  35 us
    slice x2, local copies, waits for them, and re-layouts, split_heads(): featured = short[0][None] * streams[lead:]  30.9 us
    pallas_call x1, Pallas kernels, split_heads(): pl.pallas_call(functools.partial(conv_kernel, group_w), out_shape=shape,...  27.7 us
    all_to_all x5, starting transfers between devices, exchange(): return lax.all_to_all(x, 'seq', 0, 0, tiled=True)  25.8 us
    add x1, other arithmetic, split_heads(): featured = featured + jnp.where((place >= lag)[:, None, None], term, 0.0)  17.2 us
  transfers between devices with their start and end apart: 5, of which 4 were waited for; matrix products, arithmetic and copies ran while one was open for 40% of the time, Pallas kernels for 17%

profile of v4, /device:TPU:0, one launch (start us, length us, event | category | flops | bytes accessed | tf_op | source)
XLA Modules:
  0.0 364.4 jit_solution(14112629494137740033)
XLA Ops:
  0.0 1.9 copy.41
  1.9 1.8 copy.42
  3.7 7.4 %all-to-all-start = ((f32[32,128,128]{2,1,0:T(8,128)}), f32[32,128,128]{2,1,0:T(8,128)}, u32[]{:S(2)}, u32[]{:S(2)}) async-start(f32[32,128,128]{2,1,0:T(8,128)} %bitcast.7), calls=%async_computation | async-start | bytes 4194304 | tf_op jit(solution)/shard_map/query_to_heads/all_to_all | solution.py:161
  11.2 1.9 copy.39
  13.1 1.8 copy.40
  14.9 1.9 copy.37
  16.9 1.8 copy.38
  18.9 0.3 reduce-window.9
  19.3 0.7 dynamic_slice.15
  21.0 4.7 %pad_maximum_fusion = f32[32,2,128,128]{3,2,1,0:T(8,128)} fusion(f32[32,1,128,128]{3,2,1,0:T(8,128)} %bitcast.78, f32[32,1,128,128]{3,2,1,0:T(8,128)} %bitcast.79), kind=kLoop, calls=%fused_computation.1 | loop fusion | flops 1048576 | bytes 8388608 | tf_op jit(solution)/shard_map/key_value_to_heads/stack | solution.py:177
  25.7 34.3 %all-to-all-done.q_ref = f32[32,128,128]{2,1,0:T(8,128)} async-done(((f32[32,128,128]{2,1,0:T(8,128)}), f32[32,128,128]{2,1,0:T(8,128)}, u32[]{:S(2)}, u32[]{:S(2)}) %all-to-all-start) | async-done | bytes 2097184 | tf_op jit(solution)/shard_map/query_to_heads/all_to_all | solution.py:161
  60.0 4.1 %all-to-all-start.1 = ((f32[32,2,128,128]{3,2,1,0:T(8,128)}), f32[32,2,128,128]{3,2,1,0:T(8,128)}, u32[]{:S(2)}, u32[]{:S(2)}) async-start(f32[32,2,128,128]{3,2,1,0:T(8,128)} %pad_maximum_fusion), calls=%async_computation.1 | async-start | bytes 8388608 | tf_op jit(solution)/shard_map/key_value_to_heads/all_to_all | solution.py:161
  64.2 30.9 %fusion = (f32[120,3,4096]{2,0,1:T(8,128)}, f32[120,3,4096]{2,0,1:T(8,128)}, f32[120,3,4096]{2,0,1:T(8,128)}, f32[120,3,4096]{2,0,1:T(8,128)}, f32[120,3,4096]{2...) fusion(f32[128,3,4096]{2,0,1:T(8,128)} %param.10), kind=kLoop, calls=%fused_computation.42 | loop fusion | bytes 82575360 | tf_op jit(solution)/shard_map/featured/slice | solution.py:182
  95.0 6.4 %copy.74 = f32[120,3,4096]{0,2,1:T(8,128)} copy(f32[120,3,4096]{2,0,1:T(8,128)} %get-tuple-element.31) | data formatting | bytes 11796480
  101.5 6.5 %copy.73 = f32[120,3,4096]{0,2,1:T(8,128)} copy(f32[120,3,4096]{2,0,1:T(8,128)} %get-tuple-element.26) | data formatting | bytes 11796480
  108.0 6.5 %copy.72 = f32[120,3,4096]{0,2,1:T(8,128)} copy(f32[120,3,4096]{2,0,1:T(8,128)} %get-tuple-element.27) | data formatting | bytes 11796480
  114.5 6.5 %copy.71 = f32[120,3,4096]{0,2,1:T(8,128)} copy(f32[120,3,4096]{2,0,1:T(8,128)} %get-tuple-element.28) | data formatting | bytes 11796480
  120.9 6.4 %copy.70 = f32[120,3,4096]{0,2,1:T(8,128)} copy(f32[120,3,4096]{2,0,1:T(8,128)} %get-tuple-element.29) | data formatting | bytes 11796480
  127.4 6.5 %copy.69 = f32[120,3,4096]{0,2,1:T(8,128)} copy(f32[120,3,4096]{2,0,1:T(8,128)} %get-tuple-element.30) | data formatting | bytes 11796480
  133.9 6.5 %copy.68 = f32[120,3,4096]{0,2,1:T(8,128)} copy(f32[120,3,4096]{2,0,1:T(8,128)} %get-tuple-element.25) | data formatting | bytes 11796480
  140.5 0.2 broadcast_in_dim.133
  140.7 0.2 broadcast_in_dim.134
  140.9 0.2 broadcast_in_dim.130
  141.1 0.2 broadcast_in_dim.131
  141.3 0.2 broadcast_in_dim.127
  141.5 0.2 broadcast_in_dim.128
  141.7 0.2 broadcast_in_dim.124
  141.9 0.2 broadcast_in_dim.125
  142.1 0.2 broadcast_in_dim.121
  142.3 0.2 broadcast_in_dim.122
  142.7 0.2 broadcast_in_dim.118
  143.1 0.2 broadcast_in_dim.114
  143.4 17.2 %select_add_fusion = f32[120,3,4096]{0,2,1:T(8,128)S(1)} fusion(f32[120,3,4096]{0,2,1:T(8,128)} %copy.74, f32[120,3,4096]{0,2,1:T(8,128)} %copy.73, f32[120,3,4096]{0,2,1:T(8,128)} %copy.72, f32[120,3,4096]{0,2,1:T(8,128)} %copy.71, f32[120,3,4096]{0,2,1:T(8,128)} %copy.70, f32[120,3,4096]{0,2,1:T(8,128)} %copy.69, f32[120,3,4096]{0,2,1:T(8,128)} %copy.68, ...), kind=kLoop, calls=%fused_computation | loop fusion | flops 28016640 | bytes 47530704 | tf_op jit(solution)/shard_map/featured/add | solution.py:185
  160.6 1.7 slice_bitcast_fusion
  162.3 2.9 copy.50
  165.2 3.0 constant_dynamic-update-slice_fusion
  168.2 1.6 bitcast_dynamic-update-slice_fusion.5
  169.8 1.6 bitcast_dynamic-update-slice_fusion.4
  171.4 1.6 bitcast_dynamic-update-slice_fusion.3
  173.0 1.6 bitcast_dynamic-update-slice_fusion.2
  174.5 1.6 bitcast_dynamic-update-slice_fusion.1
  176.1 1.6 bitcast_dynamic-update-slice_fusion
  177.7 5.9 %all-to-all-start.2 = ((f32[32,168,128]{2,1,0:T(8,128)}), f32[32,168,128]{2,1,0:T(8,128)}, u32[]{:S(2)}, u32[]{:S(2)}) async-start(f32[32,168,128]{2,1,0:T(8,128)} %bitcast.19), calls=%async_computation.2 | async-start | bytes 5505024 | tf_op jit(solution)/shard_map/gated_to_channels/all_to_all | solution.py:161
  183.7 2.0 copy.51.starts_ref
  185.6 0.6 select_reduce_fusion.inv_ref
  186.3 35.0 %attention.1 = f32[32,128,128]{2,1,0:T(8,128)} custom-call(s32[32]{0:T(128)} %select_reduce_fusion.inv_ref, s32[4096]{0:T(1024)} %copy-done.6, f32[32,128,128]{2,1,0:T(8,128)} %all-to-all-done.q_ref, f32[32,2,128,128]{3,2,1,0:T(8,128)} %all-to-all-done.1.kv_ref, s32[4096,1]{1,0:T(8,128)} %copy.51.starts_ref), custom_call_target="tpu_custom_call" | custom-call | flops 21474836480 | bytes 12582912 | tf_op jit(solution)/shard_map/attention/pallas_call | solution.py:218
  221.3 25.3 %all-to-all-done.2.packed_ref = f32[32,168,128]{2,1,0:T(8,128)} async-done(((f32[32,168,128]{2,1,0:T(8,128)}), f32[32,168,128]{2,1,0:T(8,128)}, u32[]{:S(2)}, u32[]{:S(2)}) %all-to-all-start.2) | async-done | bytes 2752544 | tf_op jit(solution)/shard_map/gated_to_channels/all_to_all | solution.py:161
  246.6 4.3 %all-to-all-start.3 = ((f32[32,128,128]{2,1,0:T(8,128)}), f32[32,128,128]{2,1,0:T(8,128)}, u32[]{:S(2)}, u32[]{:S(2)}) async-start(f32[32,128,128]{2,1,0:T(8,128)} %attention.1), calls=%async_computation.3 | async-start | bytes 4194304 | tf_op jit(solution)/shard_map/back_to_tokens/all_to_all | solution.py:161
  251.1 0.6 copy.54.short_ref
  252.3 1.3 slice.161
  253.6 4.2 %reshape.147 = f32[8,128,383]{2,1,0:T(8,128)} reshape(f32[8,49024]{1,0:T(8,128)} %slice.161) | data formatting | bytes 3137536 | tf_op jit(solution)/shard_map/filters/reshape | solution.py:211
  257.8 2.4 slice.162
  260.2 3.0 broadcast_in_dim.140.docs_ref
  263.2 1.5 iota_subtract_fusion.place_ref
  264.6 27.7 %conv.1 = f32[32,128,128]{2,1,0:T(8,128)} custom-call(s32[32]{0:T(128)} %select_reduce_fusion.inv_ref, s32[4096]{0:T(1024)} %doc_ref.1, f32[32,168,128]{2,1,0:T(8,128)} %all-to-all-done.2.packed_ref, f32[7,3,128]{2,1,0:T(4,128)} %copy.54.short_ref, f32[1024,256]{1,0:T(8,128)} %bitcast.81, s32[4224,1]{1,0:T(8,128)} %broadcast_in_dim.140.docs_ref, ...), custom_call_target="tpu_custom_call" | custom-call | flops 10737418240 | bytes 12582912 | tf_op jit(solution)/shard_map/conv/pallas_call | solution.py:235
  292.3 7.3 %all-to-all-done.3 = f32[32,128,128]{2,1,0:T(8,128)} async-done(((f32[32,128,128]{2,1,0:T(8,128)}), f32[32,128,128]{2,1,0:T(8,128)}, u32[]{:S(2)}, u32[]{:S(2)}) %all-to-all-start.3) | async-done | bytes 2097184 | tf_op jit(solution)/shard_map/back_to_tokens/all_to_all | solution.py:161
  299.6 4.1 %all-to-all-start.4 = ((f32[32,128,128]{2,1,0:T(8,128)}), f32[32,128,128]{2,1,0:T(8,128)}, u32[]{:S(2)}, u32[]{:S(2)}) async-start(f32[32,128,128]{2,1,0:T(8,128)} %conv.1), calls=%async_computation.4 | async-start | bytes 4194304 | tf_op jit(solution)/shard_map/back_to_tokens/all_to_all | solution.py:161
  303.7 2.9 copy.57
  306.6 46.0 %all-to-all-done.4 = f32[32,128,128]{2,1,0:T(8,128)} async-done(((f32[32,128,128]{2,1,0:T(8,128)}), f32[32,128,128]{2,1,0:T(8,128)}, u32[]{:S(2)}, u32[]{:S(2)}) %all-to-all-start.4) | async-done | bytes 2097184 | tf_op jit(solution)/shard_map/back_to_tokens/all_to_all | solution.py:161
  352.6 2.9 copy.56
  355.5 3.0 multiply_reduce_fusion
  358.5 0.5 copy-done.1
  359.0 2.5 multiply_multiply_fusion
  361.5 2.9 copy.58
  (51 shorter events, 1.9 us)
Async XLA Ops:
  3.7 56.3 %all-to-all-start = ((f32[32,128,128]{2,1,0:T(8,128)}), f32[32,128,128]{2,1,0:T(8,128)}, u32[]{:S(2)}, u32[]{:S(2)}) async-start(f32[32,128,128]{2,1,0:T(8,128)} %bitcast.7), calls=%async_computation | async-start | bytes 4194304 | tf_op jit(solution)/shard_map/query_to_heads/all_to_all | solution.py:161
  16.9 1.9 copy-start.3
  16.9 2.4 copy-start.9
  20.9 4.8 %copy-start.6 = (s32[4096]{0:T(1024)}, s32[4096]{0:T(1024)S(1)}, u32[]{:S(2)}) copy-start(s32[4096]{0:T(1024)S(1)} %fusion.2.start_ref) | copy-start | bytes 49156
  60.0 117.7 %all-to-all-start.1 = ((f32[32,2,128,128]{3,2,1,0:T(8,128)}), f32[32,2,128,128]{3,2,1,0:T(8,128)}, u32[]{:S(2)}, u32[]{:S(2)}) async-start(f32[32,2,128,128]{3,2,1,0:T(8,128)} %pad_maximum_fusion), calls=%async_computation.1 | async-start | bytes 8388608 | tf_op jit(solution)/shard_map/key_value_to_heads/all_to_all | solution.py:161
  133.9 6.5 %copy-start.4 = (f32[7,3,256]{2,0,1:T(8,128)S(1)}, f32[7,3,256]{2,0,1:T(8,128)}, u32[]{:S(2)}) copy-start(f32[7,3,256]{2,0,1:T(8,128)} %param.11) | copy-start | bytes 64516
  177.7 68.9 %all-to-all-start.2 = ((f32[32,168,128]{2,1,0:T(8,128)}), f32[32,168,128]{2,1,0:T(8,128)}, u32[]{:S(2)}, u32[]{:S(2)}) async-start(f32[32,168,128]{2,1,0:T(8,128)} %bitcast.19), calls=%async_computation.2 | async-start | bytes 5505024 | tf_op jit(solution)/shard_map/gated_to_channels/all_to_all | solution.py:161
  221.3 30.5 %copy-start.8 = (f32[256]{0:T(256)S(1)}, f32[256]{0:T(256)}, u32[]{:S(2)}) copy-start(f32[256]{0:T(256)} %param.13) | copy-start | bytes 3076
  221.3 30.6 %copy-start.5 = (f32[128,256]{1,0:T(8,128)S(1)}, f32[128,256]{1,0:T(8,128)}, u32[]{:S(2)}) copy-start(f32[128,256]{1,0:T(8,128)} %param.12) | copy-start | bytes 393220
  246.6 53.0 %all-to-all-start.3 = ((f32[32,128,128]{2,1,0:T(8,128)}), f32[32,128,128]{2,1,0:T(8,128)}, u32[]{:S(2)}, u32[]{:S(2)}) async-start(f32[32,128,128]{2,1,0:T(8,128)} %attention.1), calls=%async_computation.3 | async-start | bytes 4194304 | tf_op jit(solution)/shard_map/back_to_tokens/all_to_all | solution.py:161
  257.8 5.4 %copy-start.2 = (s32[4096,1]{1,0:T(8,128)S(1)}, s32[4096,1]{1,0:T(8,128)}, u32[]{:S(2)}) copy-start(s32[4096,1]{1,0:T(8,128)} %copy.51.starts_ref) | copy-start | bytes 49156
  299.6 53.0 %all-to-all-start.4 = ((f32[32,128,128]{2,1,0:T(8,128)}), f32[32,128,128]{2,1,0:T(8,128)}, u32[]{:S(2)}, u32[]{:S(2)}) async-start(f32[32,128,128]{2,1,0:T(8,128)} %conv.1), calls=%async_computation.4 | async-start | bytes 4194304 | tf_op jit(solution)/shard_map/back_to_tokens/all_to_all | solution.py:161
  355.5 3.0 copy-start
  355.5 3.5 copy-start.1
  355.5 3.5 copy-start.7
